TPU v7x, 512 devices: a whole 4x8x8 slice. The times are simulated.
512 devices in a mesh: pipe: 8 (over y_lo, core), ctx: 32 (over x, z), dp: 2 (over y_hi).
Axes of the slice: x: 4, y: 8 (y_hi: 2, y_lo: 4; y = y_hi * 4 + y_lo), z: 8, core: 2. Of those that a mesh axis runs over, the one named last changes fastest.
Arguments:
- section_queries: bfloat16 [8, 8192, 4096], P('pipe', ('ctx', 'dp')), may hold values from -20 to 20
- section_keys: bfloat16 [8, 8192, 512], P('pipe', ('ctx', 'dp')), may hold values from -20 to 20
- cascade_value_rows: bfloat16 [8, 8192, 512], P('pipe', ('ctx', 'dp')), may hold values from -6 to 6
- output_grad: bfloat16 [8, 8192, 4096], P('pipe', ('ctx', 'dp')), may hold values from -6 to 6
- segments: int32 [8192], replicated, may hold values from 0 to 53, never falling along the last dimension, each value on 1 to 448 neighbouring positions
- stretch_plan: int32 [128], replicated, may hold values from 0 to 127, as said below
Outputs:
- section_output: bfloat16 [8, 8192, 4096], P('pipe', ('ctx', 'dp'))
- query_grad_sent: bfloat16 [8, 8192, 4096], P('pipe', ('ctx', 'dp'))
- key_grad: bfloat16 [8, 8192, 512], P('pipe', ('ctx', 'dp'))
- value_grad: bfloat16 [8, 8192, 512], P('pipe', ('ctx', 'dp'))
Inputs may be any that keep to these rules, and one draw needn't show every extreme that they name: `stretch_plan`: A permutation of the 128 half-blocks. Slots 2 * i and 2 * i + 1 belong to index i of ctx+dp; each holds one of that index's own two half-blocks or the half-block of a neighbouring index that adjoins index i's tokens.
All inputs are finite; a program needn't handle non-finite values.
Results may differ from a plain program's by a relative error of at most 0.012.
The roundings to bfloat16 on the way count: a program that leaves them out, or rounds other values in their place, can miss the bound.
Values may be sent and summed in bfloat16 or wider, within the bound.
A program may use at most 64 MiB of HBM per device.

v0:
```python
import math

import jax
import jax.numpy as jnp
from jax import lax
from jax.sharding import PartitionSpec as P

QUERY_HEADS = 32
KEY_VALUE_HEADS = 4
HEAD_SIZE = 128
NBACK = 4


def extended(cells, sides, width):
    for axis, dim in sides:
        count = lax.axis_size(axis)
        ends = count - 1
        head = lax.slice_in_dim(cells, 0, width, axis=dim)
        tail = lax.slice_in_dim(cells, cells.shape[dim] - width, cells.shape[dim], axis=dim)
        cells = jnp.concatenate(
            [
                lax.ppermute(tail, axis, [(i, (i + 1) % count) for i in range(ends)]),
                cells,
                lax.ppermute(head, axis, [((i + 1) % count, i) for i in range(ends)]),
            ],
            axis=dim,
        )
    return cells


def from_behind(value, axis, by):
    count = lax.axis_size(axis)
    pairs = [(i, i + by) for i in range(count) if 0 <= i + by < count]
    return lax.ppermute(value, axis, pairs)


def on_device(
    section_queries, section_keys, cascade_value_rows, output_grad, segments, stretch_plan
):
    tokens_here = section_queries.shape[1]
    half_block_rows = tokens_here // 2
    width = section_queries.shape[2]
    kv_width = section_keys.shape[2]
    head_groupings = QUERY_HEADS // KEY_VALUE_HEADS
    scaling = 1.0 / math.sqrt(HEAD_SIZE)
    device = lax.axis_index(("ctx", "dp"))
    window_extent = NBACK
    span = (window_extent + 2) * tokens_here
    rimmed = extended(section_queries[0], ((("ctx", "dp"), 0),), half_block_rows)
    slot_pair = lax.dynamic_slice_in_dim(stretch_plan, 2 * device, 2)
    picked = []
    query_pos = []
    query_seg = []
    for which in range(2):
        block = slot_pair[which]
        picked.append(
            lax.dynamic_slice_in_dim(
                rimmed, (block - 2 * device + 1) * half_block_rows, half_block_rows, 0
            )
        )
        query_pos.append(block * half_block_rows + jnp.arange(half_block_rows, dtype=jnp.int32))
        query_seg.append(
            lax.dynamic_slice_in_dim(segments, block * half_block_rows, half_block_rows)
        )
    chosen = jnp.concatenate(picked, axis=0)
    query_pos = jnp.concatenate(query_pos)
    query_seg = jnp.concatenate(query_seg)
    paired = jnp.stack([section_keys[0], cascade_value_rows[0]])
    offsets = list(range(window_extent, -2, -1))
    blocks = [
        paired if offset == 0 else from_behind(paired, ("ctx", "dp"), offset) for offset in offsets
    ]
    window = jnp.concatenate(blocks, axis=1)
    first_pos = (device - window_extent) * tokens_here
    key_pos = first_pos + jnp.arange(span, dtype=jnp.int32)
    padded_seg = jnp.pad(segments, (window_extent * tokens_here, tokens_here), constant_values=-1)
    key_seg = lax.dynamic_slice_in_dim(padded_seg, first_pos + window_extent * tokens_here, span)
    visible = (query_seg[:, None] == key_seg[None, :]) & (key_pos[None, :] <= query_pos[:, None])
    grads_here = output_grad[0]

    def single_grouping(index):
        query_group = lax.dynamic_slice_in_dim(
            chosen, index * head_groupings * HEAD_SIZE, head_groupings * HEAD_SIZE, 1
        ).reshape(tokens_here, head_groupings, HEAD_SIZE)
        grad_group = lax.dynamic_slice_in_dim(
            grads_here, index * head_groupings * HEAD_SIZE, head_groupings * HEAD_SIZE, 1
        ).reshape(tokens_here, head_groupings, HEAD_SIZE)
        key_group = lax.dynamic_slice_in_dim(window[0], index * HEAD_SIZE, HEAD_SIZE, 1)
        value_group = lax.dynamic_slice_in_dim(window[1], index * HEAD_SIZE, HEAD_SIZE, 1)
        scores = (
            jnp.einsum("iha,ja->hij", query_group, key_group, preferred_element_type=jnp.float32)
            * scaling
        )
        scores = jnp.where(visible[None], scores, -jnp.inf)
        top = jnp.max(scores, axis=-1, keepdims=True)
        weights = jnp.exp(scores - top)
        probs = weights / jnp.sum(weights, axis=-1, keepdims=True)
        probs_low = probs.astype(jnp.bfloat16)
        attended = jnp.einsum(
            "hij,ja->iha", probs_low, value_group, preferred_element_type=jnp.float32
        ).astype(jnp.bfloat16)
        grad_probs = jnp.einsum(
            "iha,ja->hij", grad_group, value_group, preferred_element_type=jnp.float32
        )
        delta = jnp.sum(grad_group.astype(jnp.float32) * attended.astype(jnp.float32), axis=2)
        grad_scores = (probs * (grad_probs - jnp.transpose(delta)[:, :, None])).astype(jnp.bfloat16)
        query_grad = (
            jnp.einsum("hij,ja->iha", grad_scores, key_group, preferred_element_type=jnp.float32)
            * scaling
        ).astype(jnp.bfloat16)
        key_portion = (
            jnp.einsum("hij,iha->ja", grad_scores, query_group, preferred_element_type=jnp.float32)
            * scaling
        )
        value_portion = jnp.einsum(
            "hij,iha->ja", probs_low, grad_group, preferred_element_type=jnp.float32
        )
        return (
            attended.reshape(tokens_here, head_groupings * HEAD_SIZE),
            query_grad.reshape(tokens_here, head_groupings * HEAD_SIZE),
            key_portion,
            value_portion,
        )

    attended, query_grad, key_parts, value_parts = lax.map(
        single_grouping, jnp.arange(KEY_VALUE_HEADS, dtype=jnp.int32)
    )
    attended = jnp.transpose(attended, (1, 0, 2)).reshape(tokens_here, width)
    query_grad = jnp.transpose(query_grad, (1, 0, 2)).reshape(tokens_here, width)
    key_parts = jnp.transpose(key_parts, (1, 0, 2)).reshape(span, kv_width)
    value_parts = jnp.transpose(value_parts, (1, 0, 2)).reshape(span, kv_width)
    partial_grads = jnp.stack([key_parts, value_parts])

    def piece(offset):
        begin = (window_extent - offset) * tokens_here
        return partial_grads[:, begin : begin + tokens_here]

    summed = piece(0)
    for offset in offsets:
        if offset != 0:
            summed = summed + from_behind(piece(offset), ("ctx", "dp"), -offset)
    section_output = from_behind(attended[None], "pipe", 1)
    query_grad_sent = from_behind(query_grad[None], "pipe", -1)
    key_grad = summed[0].astype(jnp.bfloat16)[None]
    value_grad = summed[1].astype(jnp.bfloat16)[None]
    return (section_output, query_grad_sent, key_grad, value_grad)


def solution(mesh):
    placed = (
        P("pipe", ("ctx", "dp"), None),
        P("pipe", ("ctx", "dp"), None),
        P("pipe", ("ctx", "dp"), None),
        P("pipe", ("ctx", "dp"), None),
        P(),
        P(),
    )
    return jax.shard_map(
        on_device,
        mesh=mesh,
        in_specs=placed,
        out_specs=(
            P("pipe", ("ctx", "dp"), None),
            P("pipe", ("ctx", "dp"), None),
            P("pipe", ("ctx", "dp"), None),
            P("pipe", ("ctx", "dp"), None),
        ),
        check_vma=False,
    )
```

profile of v0, /device:TPU:94, one launch (start us, length us, event | category | flops | bytes accessed | tf_op | source)
XLA Modules:
  0.0 286.9 jit_solution(18236624097503497799)
XLA Ops:
  0.7 1.7 constant_dynamic-update-slice_fusion.3
  2.3 1.6 constant_dynamic-update-slice_fusion.2
  3.9 6.1 %collective-permute-start = (bf16[2,128,512]{2,1,0:T(8,128)(2,1)}, bf16[2,128,512]{2,1,0:T(8,128)(2,1)S(1)}, u32[]{:S(2)}, u32[]{:S(2)}) collective-permute-start(bf16[2,128,512]{2,1,0:T(8,128)(2,1)} %constant_dynamic-update-slice_fusion.2), channel_id=1, source_target_pairs={{0,4},{1,5},{2,6},{3,7},{4,8},{5,9},{6,10},{7,11},{8,12},{9,13},{1... | collective-permute-start | bytes 786440 | tf_op jit(solution)/shard_map/ppermute | solution.py:34
  10.0 8.1 %collective-permute-start.1 = (bf16[2,128,512]{2,1,0:T(8,128)(2,1)}, bf16[2,128,512]{2,1,0:T(8,128)(2,1)}, u32[]{:S(2)}, u32[]{:S(2)}) collective-permute-start(bf16[2,128,512]{2,1,0:T(8,128)(2,1)} %constant_dynamic-update-slice_fusion.2), channel_id=1, source_target_pairs={{0,3},{1,4},{2,5},{3,6},{4,7},{5,8},{6,9},{7,10},{8,11},{9,12},{10... | collective-permute-start | bytes 786440 | tf_op jit(solution)/shard_map/ppermute | solution.py:34
  18.0 3.4 %collective-permute-start.2 = (bf16[2,128,512]{2,1,0:T(8,128)(2,1)}, bf16[2,128,512]{2,1,0:T(8,128)(2,1)}, u32[]{:S(2)}, u32[]{:S(2)}) collective-permute-start(bf16[2,128,512]{2,1,0:T(8,128)(2,1)} %constant_dynamic-update-slice_fusion.2), channel_id=1, source_target_pairs={{0,2},{1,3},{2,4},{3,5},{4,6},{5,7},{6,8},{7,9},{8,10},{9,11},{10,... | collective-permute-start | bytes 786440 | tf_op jit(solution)/shard_map/ppermute | solution.py:34
  21.4 5.6 %collective-permute-start.3 = (bf16[2,128,512]{2,1,0:T(8,128)(2,1)}, bf16[2,128,512]{2,1,0:T(8,128)(2,1)}, u32[]{:S(2)}, u32[]{:S(2)}) collective-permute-start(bf16[2,128,512]{2,1,0:T(8,128)(2,1)} %constant_dynamic-update-slice_fusion.2), channel_id=1, source_target_pairs={{0,1},{1,2},{2,3},{3,4},{4,5},{5,6},{6,7},{7,8},{8,9},{9,10},{10,1... | collective-permute-start | bytes 786440 | tf_op jit(solution)/shard_map/ppermute | solution.py:34
  27.1 5.0 %collective-permute-start.4 = (bf16[2,128,512]{2,1,0:T(8,128)(2,1)}, bf16[2,128,512]{2,1,0:T(8,128)(2,1)}, u32[]{:S(2)}, u32[]{:S(2)}) collective-permute-start(bf16[2,128,512]{2,1,0:T(8,128)(2,1)} %constant_dynamic-update-slice_fusion.2), channel_id=1, source_target_pairs={{1,0},{2,1},{3,2},{4,3},{5,4},{6,5},{7,6},{8,7},{9,8},{10,9},{11,1... | collective-permute-start | bytes 786440 | tf_op jit(solution)/shard_map/ppermute | solution.py:34
  34.7 2.3 slice_bitcast_fusion.1
  39.4 2.3 copy.51
  41.7 1.7 collective-permute-done
  44.1 3.0 %collective-permute-start.5 = (bf16[64,4096]{1,0:T(8,128)(2,1)}, bf16[64,4096]{1,0:T(8,128)(2,1)S(1)}, u32[]{:S(2)}, u32[]{:S(2)}) collective-permute-start(bf16[64,4096]{1,0:T(8,128)(2,1)} %get-tuple-element.209), channel_id=1, source_target_pairs={{0,1},{1,2},{2,3},{3,4},{4,5},{5,6},{6,7},{7,8},{8,9},{9,10},{10,1... | collective-permute-start | bytes 1572872 | tf_op jit(solution)/shard_map/ppermute | solution.py:22
  48.1 7.6 %collective-permute-start.6 = (bf16[64,4096]{1,0:T(8,128)(2,1)}, bf16[64,4096]{1,0:T(8,128)(2,1)}, u32[]{:S(2)}, u32[]{:S(2)}) collective-permute-start(bf16[64,4096]{1,0:T(8,128)(2,1)} %get-tuple-element.210), channel_id=1, source_target_pairs={{1,0},{2,1},{3,2},{4,3},{5,4},{6,5},{7,6},{8,7},{9,8},{10,9},{11,1... | collective-permute-start | bytes 1572872 | tf_op jit(solution)/shard_map/ppermute | solution.py:24
  58.7 2.0 collective-permute-done.4
  61.6 25.9 %collective-permute-done.5 = bf16[64,4096]{1,0:T(8,128)(2,1)S(1)} collective-permute-done((bf16[64,4096]{1,0:T(8,128)(2,1)}, bf16[64,4096]{1,0:T(8,128)(2,1)S(1)}, u32[]{:S(2)}, u32[]{:S(2)}) %collective-permute-start.5) | collective-permute-done | bytes 524320 | tf_op jit(solution)/shard_map/ppermute | solution.py:22
  87.5 1.3 copy.49
  88.8 12.0 %collective-permute-done.6 = bf16[64,4096]{1,0:T(8,128)(2,1)} collective-permute-done((bf16[64,4096]{1,0:T(8,128)(2,1)}, bf16[64,4096]{1,0:T(8,128)(2,1)}, u32[]{:S(2)}, u32[]{:S(2)}) %collective-permute-start.6) | collective-permute-done | bytes 524320 | tf_op jit(solution)/shard_map/ppermute | solution.py:24
  100.9 2.4 copy.50
  103.2 2.7 pad_maximum_fusion
  107.2 55.1 %while.19 = (s32[]{:T(128)}, bf16[4,128,1024]{1,2,0:T(8,128)(2,1)}, bf16[4,128,1024]{1,2,0:T(8,128)(2,1)}, f32[4,768,128]{2,1,0:T(8,128)}, f32[4,768,128]{2,1,0:...) while((s32[]{:T(128)}, bf16[4,128,1024]{1,2,0:T(8,128)(2,1)}, ...), condition=%wide.region_4.5_spmd.clone, body=%wide.region_0.4_spmd.clone.sunk | while | flops 1217134336 | bytes 51868600 | solution.py:125
  109.6 1.3 fusion.98
  110.9 2.0 fusion.99
  114.5 1.0 multiply_reduce_fusion.2
  115.5 1.4 fusion.104
  117.5 1.3 fusion.102
  119.7 1.3 fusion.103
  123.3 1.3 fusion.98
  124.7 2.0 fusion.99
  128.2 1.0 multiply_reduce_fusion.2
  129.3 1.3 fusion.104
  131.2 1.3 fusion.102
  133.4 1.3 fusion.103
  137.1 1.3 fusion.98
  138.4 2.0 fusion.99
  142.0 1.0 multiply_reduce_fusion.2
  143.0 1.3 fusion.104
  145.0 1.3 fusion.102
  147.2 1.3 fusion.103
  150.8 1.3 fusion.98
  152.2 2.0 fusion.99
  155.8 1.0 multiply_reduce_fusion.2
  156.8 1.3 fusion.104
  158.7 1.3 fusion.102
  160.9 1.3 fusion.103
  162.3 2.4 copy.54
  164.7 1.8 stack_reshape.6
  166.5 1.6 constant_dynamic-update-slice_fusion.12
  168.4 2.2 copy.55
  170.6 2.8 stack_reshape.7
  173.4 1.5 constant_dynamic-update-slice_fusion.11
  174.9 1.5 fusion.54
  176.4 6.2 %collective-permute-start.10 = (f32[2,128,512]{2,1,0:T(8,128)}, f32[2,128,512]{2,1,0:T(8,128)}, u32[]{:S(2)}, u32[]{:S(2)}) collective-permute-start(f32[2,128,512]{2,1,0:T(8,128)} %get-tuple-element.206), channel_id=1, source_target_pairs={{3,0},{4,1},{5,2},{6,3},{7,4},{8,5},{9,6},{10,7},{11,8},{12,9},{13... | collective-permute-start | bytes 1572872 | tf_op jit(solution)/shard_map/ppermute | solution.py:34
  182.6 3.0 %collective-permute-start.11 = (f32[2,128,512]{2,1,0:T(8,128)}, f32[2,128,512]{2,1,0:T(8,128)}, u32[]{:S(2)}, u32[]{:S(2)}) collective-permute-start(f32[2,128,512]{2,1,0:T(8,128)} %get-tuple-element.205), channel_id=1, source_target_pairs={{2,0},{3,1},{4,2},{5,3},{6,4},{7,5},{8,6},{9,7},{10,8},{11,9},{12,... | collective-permute-start | bytes 1572872 | tf_op jit(solution)/shard_map/ppermute | solution.py:34
  185.6 7.5 %collective-permute-start.12 = (f32[2,128,512]{2,1,0:T(8,128)}, f32[2,128,512]{2,1,0:T(8,128)}, u32[]{:S(2)}, u32[]{:S(2)}) collective-permute-start(f32[2,128,512]{2,1,0:T(8,128)} %get-tuple-element.204), channel_id=1, source_target_pairs={{1,0},{2,1},{3,2},{4,3},{5,4},{6,5},{7,6},{8,7},{9,8},{10,9},{11,1... | collective-permute-start | bytes 1572872 | tf_op jit(solution)/shard_map/ppermute | solution.py:34
  193.1 2.2 collective-permute-start.13
  195.4 2.1 collective-permute-start.9
  197.5 2.3 copy.64
  199.8 2.3 copy.65
  202.0 28.9 %collective-permute-done.10 = f32[2,128,512]{2,1,0:T(8,128)} collective-permute-done((f32[2,128,512]{2,1,0:T(8,128)}, f32[2,128,512]{2,1,0:T(8,128)}, u32[]{:S(2)}, u32[]{:S(2)}) %collective-permute-start.10) | collective-permute-done | bytes 524320 | tf_op jit(solution)/shard_map/ppermute | solution.py:34
  230.9 1.9 collective-permute-start.7
  232.8 6.2 %collective-permute-start.8 = (bf16[1,128,4096]{2,1,0:T(8,128)(2,1)}, bf16[1,128,4096]{2,1,0:T(8,128)(2,1)S(1)}, u32[]{:S(2)}, u32[]{:S(2)}) collective-permute-start(bf16[1,128,4096]{2,1,0:T(8,128)(2,1)} %copy.65), channel_id=1, source_target_pairs={{64,0},{128,64},{192,128},{256,192},{320,256},{384,320},{448,384},... | collective-permute-start | bytes 3145736 | tf_op jit(solution)/shard_map/ppermute | solution.py:34
  239.0 6.1 %collective-permute-done.12 = f32[2,128,512]{2,1,0:T(8,128)} collective-permute-done((f32[2,128,512]{2,1,0:T(8,128)}, f32[2,128,512]{2,1,0:T(8,128)}, u32[]{:S(2)}, u32[]{:S(2)}) %collective-permute-start.12) | collective-permute-done | bytes 524320 | tf_op jit(solution)/shard_map/ppermute | solution.py:34
  245.2 11.1 %collective-permute-done.13 = f32[2,128,512]{2,1,0:T(8,128)} collective-permute-done((f32[2,128,512]{2,1,0:T(8,128)}, f32[2,128,512]{2,1,0:T(8,128)}, u32[]{:S(2)}, u32[]{:S(2)}) %collective-permute-start.13) | collective-permute-done | bytes 524320 | tf_op jit(solution)/shard_map/ppermute | solution.py:34
  256.3 2.0 fusion.47
  259.0 26.0 %collective-permute-done.7 = bf16[1,128,4096]{2,1,0:T(8,128)(2,1)S(1)} collective-permute-done((bf16[1,128,4096]{2,1,0:T(8,128)(2,1)}, bf16[1,128,4096]{2,1,0:T(8,128)(2,1)S(1)}, u32[]{:S(2)}, u32[]{:S(2)}) %collective-permute-start.7) | collective-permute-done | bytes 1048608 | tf_op jit(solution)/shard_map/ppermute | solution.py:34
  (111 shorter events, 27.8 us)
Async XLA Ops:
  0.6 38.0 %copy-start.5 = (bf16[1,128,4096]{2,1,0:T(8,128)(2,1)S(1)}, bf16[1,128,4096]{2,1,0:T(8,128)(2,1)}, u32[]{:S(2)}) copy-start(bf16[1,128,4096]{2,1,0:T(8,128)(2,1)} %param.8) | copy-start | bytes 3145732
  0.6 36.4 %copy-start.10 = (s32[8192]{0:T(1024)S(1)}, s32[8192]{0:T(1024)}, u32[]{:S(2)}) copy-start(s32[8192]{0:T(1024)} %param.12) | copy-start | bytes 98308
  3.9 39.5 %collective-permute-start = (bf16[2,128,512]{2,1,0:T(8,128)(2,1)}, bf16[2,128,512]{2,1,0:T(8,128)(2,1)S(1)}, u32[]{:S(2)}, u32[]{:S(2)}) collective-permute-start(bf16[2,128,512]{2,1,0:T(8,128)(2,1)} %constant_dynamic-update-slice_fusion.2), channel_id=1, source_target_pairs={{0,4},{1,5},{2,6},{3,7},{4,8},{5,9},{6,10},{7,11},{8,12},{9,13},{1... | collective-permute-start | bytes 786440 | tf_op jit(solution)/shard_map/ppermute | solution.py:34
  10.0 38.1 %collective-permute-start.1 = (bf16[2,128,512]{2,1,0:T(8,128)(2,1)}, bf16[2,128,512]{2,1,0:T(8,128)(2,1)}, u32[]{:S(2)}, u32[]{:S(2)}) collective-permute-start(bf16[2,128,512]{2,1,0:T(8,128)(2,1)} %constant_dynamic-update-slice_fusion.2), channel_id=1, source_target_pairs={{0,3},{1,4},{2,5},{3,6},{4,7},{5,8},{6,9},{7,10},{8,11},{9,12},{10... | collective-permute-start | bytes 786440 | tf_op jit(solution)/shard_map/ppermute | solution.py:34
  18.0 38.6 %collective-permute-start.2 = (bf16[2,128,512]{2,1,0:T(8,128)(2,1)}, bf16[2,128,512]{2,1,0:T(8,128)(2,1)}, u32[]{:S(2)}, u32[]{:S(2)}) collective-permute-start(bf16[2,128,512]{2,1,0:T(8,128)(2,1)} %constant_dynamic-update-slice_fusion.2), channel_id=1, source_target_pairs={{0,2},{1,3},{2,4},{3,5},{4,6},{5,7},{6,8},{7,9},{8,10},{9,11},{10,... | collective-permute-start | bytes 786440 | tf_op jit(solution)/shard_map/ppermute | solution.py:34
  21.4 36.2 %collective-permute-start.3 = (bf16[2,128,512]{2,1,0:T(8,128)(2,1)}, bf16[2,128,512]{2,1,0:T(8,128)(2,1)}, u32[]{:S(2)}, u32[]{:S(2)}) collective-permute-start(bf16[2,128,512]{2,1,0:T(8,128)(2,1)} %constant_dynamic-update-slice_fusion.2), channel_id=1, source_target_pairs={{0,1},{1,2},{2,3},{3,4},{4,5},{5,6},{6,7},{7,8},{8,9},{9,10},{10,1... | collective-permute-start | bytes 786440 | tf_op jit(solution)/shard_map/ppermute | solution.py:34
  27.1 33.6 %collective-permute-start.4 = (bf16[2,128,512]{2,1,0:T(8,128)(2,1)}, bf16[2,128,512]{2,1,0:T(8,128)(2,1)}, u32[]{:S(2)}, u32[]{:S(2)}) collective-permute-start(bf16[2,128,512]{2,1,0:T(8,128)(2,1)} %constant_dynamic-update-slice_fusion.2), channel_id=1, source_target_pairs={{1,0},{2,1},{3,2},{4,3},{5,4},{6,5},{7,6},{8,7},{9,8},{10,9},{11,1... | collective-permute-start | bytes 786440 | tf_op jit(solution)/shard_map/ppermute | solution.py:34
  41.7 17.0 %copy-start.7 = (bf16[1,128,512]{2,1,0:T(8,128)(2,1)S(1)}, bf16[1,128,512]{2,1,0:T(8,128)(2,1)}, u32[]{:S(2)}) copy-start(bf16[1,128,512]{2,1,0:T(8,128)(2,1)} %param.9) | copy-start | bytes 393220
  41.7 17.0 %copy-start.8 = (bf16[1,128,512]{2,1,0:T(8,128)(2,1)S(1)}, bf16[1,128,512]{2,1,0:T(8,128)(2,1)}, u32[]{:S(2)}) copy-start(bf16[1,128,512]{2,1,0:T(8,128)(2,1)} %param.10) | copy-start | bytes 393220
  43.4 0.7 copy-start.9
  44.1 43.5 %collective-permute-start.5 = (bf16[64,4096]{1,0:T(8,128)(2,1)}, bf16[64,4096]{1,0:T(8,128)(2,1)S(1)}, u32[]{:S(2)}, u32[]{:S(2)}) collective-permute-start(bf16[64,4096]{1,0:T(8,128)(2,1)} %get-tuple-element.209), channel_id=1, source_target_pairs={{0,1},{1,2},{2,3},{3,4},{4,5},{5,6},{6,7},{7,8},{8,9},{9,10},{10,1... | collective-permute-start | bytes 1572872 | tf_op jit(solution)/shard_map/ppermute | solution.py:22
  48.1 52.8 %collective-permute-start.6 = (bf16[64,4096]{1,0:T(8,128)(2,1)}, bf16[64,4096]{1,0:T(8,128)(2,1)}, u32[]{:S(2)}, u32[]{:S(2)}) collective-permute-start(bf16[64,4096]{1,0:T(8,128)(2,1)} %get-tuple-element.210), channel_id=1, source_target_pairs={{1,0},{2,1},{3,2},{4,3},{5,4},{6,5},{7,6},{8,7},{9,8},{10,9},{11,1... | collective-permute-start | bytes 1572872 | tf_op jit(solution)/shard_map/ppermute | solution.py:24
  107.2 3.7 %copy-start = (bf16[2,768,512]{2,1,0:T(8,128)(2,1)}, bf16[2,768,512]{2,1,0:T(8,128)(2,1)S(1)}, u32[]{:S(2)}) copy-start(bf16[2,768,512]{2,1,0:T(8,128)(2,1)S(1)} %get-tuple-element.359) | copy-start | bytes 4718596 | tf_op jit(solution)/shard_map/while
  107.2 3.7 %copy-start.3 = (bf16[128,4096]{0,1:T(8,128)(2,1)}, bf16[128,4096]{0,1:T(8,128)(2,1)S(1)}, u32[]{:S(2)}) copy-start(bf16[128,4096]{0,1:T(8,128)(2,1)S(1)} %get-tuple-element.361) | copy-start | bytes 3145732 | tf_op jit(solution)/shard_map/while
  112.9 1.1 copy-start.2
  118.8 2.2 copy-start.1
  119.7 1.3 copy-start.4
  121.0 3.6 %copy-start = (bf16[2,768,512]{2,1,0:T(8,128)(2,1)}, bf16[2,768,512]{2,1,0:T(8,128)(2,1)S(1)}, u32[]{:S(2)}) copy-start(bf16[2,768,512]{2,1,0:T(8,128)(2,1)S(1)} %get-tuple-element.359) | copy-start | bytes 4718596 | tf_op jit(solution)/shard_map/while
  121.0 3.6 %copy-start.3 = (bf16[128,4096]{0,1:T(8,128)(2,1)}, bf16[128,4096]{0,1:T(8,128)(2,1)S(1)}, u32[]{:S(2)}) copy-start(bf16[128,4096]{0,1:T(8,128)(2,1)S(1)} %get-tuple-element.361) | copy-start | bytes 3145732 | tf_op jit(solution)/shard_map/while
  126.7 1.1 copy-start.2
  132.6 2.2 copy-start.1
  133.4 1.3 copy-start.4
  134.7 3.6 %copy-start = (bf16[2,768,512]{2,1,0:T(8,128)(2,1)}, bf16[2,768,512]{2,1,0:T(8,128)(2,1)S(1)}, u32[]{:S(2)}) copy-start(bf16[2,768,512]{2,1,0:T(8,128)(2,1)S(1)} %get-tuple-element.359) | copy-start | bytes 4718596 | tf_op jit(solution)/shard_map/while
  134.7 3.6 %copy-start.3 = (bf16[128,4096]{0,1:T(8,128)(2,1)}, bf16[128,4096]{0,1:T(8,128)(2,1)S(1)}, u32[]{:S(2)}) copy-start(bf16[128,4096]{0,1:T(8,128)(2,1)S(1)} %get-tuple-element.361) | copy-start | bytes 3145732 | tf_op jit(solution)/shard_map/while
  140.4 1.1 copy-start.2
  146.3 2.2 copy-start.1
  147.2 1.3 copy-start.4
  148.5 3.7 %copy-start = (bf16[2,768,512]{2,1,0:T(8,128)(2,1)}, bf16[2,768,512]{2,1,0:T(8,128)(2,1)S(1)}, u32[]{:S(2)}) copy-start(bf16[2,768,512]{2,1,0:T(8,128)(2,1)S(1)} %get-tuple-element.359) | copy-start | bytes 4718596 | tf_op jit(solution)/shard_map/while
  148.5 3.7 %copy-start.3 = (bf16[128,4096]{0,1:T(8,128)(2,1)}, bf16[128,4096]{0,1:T(8,128)(2,1)S(1)}, u32[]{:S(2)}) copy-start(bf16[128,4096]{0,1:T(8,128)(2,1)S(1)} %get-tuple-element.361) | copy-start | bytes 3145732 | tf_op jit(solution)/shard_map/while
  154.2 1.1 copy-start.2
  160.1 2.2 copy-start.1
  160.9 1.3 copy-start.4
  166.5 1.9 copy-start.6
  176.4 54.5 %collective-permute-start.10 = (f32[2,128,512]{2,1,0:T(8,128)}, f32[2,128,512]{2,1,0:T(8,128)}, u32[]{:S(2)}, u32[]{:S(2)}) collective-permute-start(f32[2,128,512]{2,1,0:T(8,128)} %get-tuple-element.206), channel_id=1, source_target_pairs={{3,0},{4,1},{5,2},{6,3},{7,4},{8,5},{9,6},{10,7},{11,8},{12,9},{13... | collective-permute-start | bytes 1572872 | tf_op jit(solution)/shard_map/ppermute | solution.py:34
  182.6 50.2 %collective-permute-start.11 = (f32[2,128,512]{2,1,0:T(8,128)}, f32[2,128,512]{2,1,0:T(8,128)}, u32[]{:S(2)}, u32[]{:S(2)}) collective-permute-start(f32[2,128,512]{2,1,0:T(8,128)} %get-tuple-element.205), channel_id=1, source_target_pairs={{2,0},{3,1},{4,2},{5,3},{6,4},{7,5},{8,6},{9,7},{10,8},{11,9},{12,... | collective-permute-start | bytes 1572872 | tf_op jit(solution)/shard_map/ppermute | solution.py:34
  185.6 59.6 %collective-permute-start.12 = (f32[2,128,512]{2,1,0:T(8,128)}, f32[2,128,512]{2,1,0:T(8,128)}, u32[]{:S(2)}, u32[]{:S(2)}) collective-permute-start(f32[2,128,512]{2,1,0:T(8,128)} %get-tuple-element.204), channel_id=1, source_target_pairs={{1,0},{2,1},{3,2},{4,3},{5,4},{6,5},{7,6},{8,7},{9,8},{10,9},{11,1... | collective-permute-start | bytes 1572872 | tf_op jit(solution)/shard_map/ppermute | solution.py:34
  193.1 63.2 %collective-permute-start.13 = (f32[2,128,512]{2,1,0:T(8,128)}, f32[2,128,512]{2,1,0:T(8,128)}, u32[]{:S(2)}, u32[]{:S(2)}) collective-permute-start(f32[2,128,512]{2,1,0:T(8,128)} %get-tuple-element.203), channel_id=1, source_target_pairs={{0,1},{1,2},{2,3},{3,4},{4,5},{5,6},{6,7},{7,8},{8,9},{9,10},{10,1... | collective-permute-start | bytes 1572872 | tf_op jit(solution)/shard_map/ppermute | solution.py:34
  195.4 60.9 %collective-permute-start.9 = (f32[2,128,512]{2,1,0:T(8,128)}, f32[2,128,512]{2,1,0:T(8,128)}, u32[]{:S(2)}, u32[]{:S(2)}) collective-permute-start(f32[2,128,512]{2,1,0:T(8,128)} %get-tuple-element.202), channel_id=1, source_target_pairs={{4,0},{5,1},{6,2},{7,3},{8,4},{9,5},{10,6},{11,7},{12,8},{13,9},{1... | collective-permute-start | bytes 1572872 | tf_op jit(solution)/shard_map/ppermute | solution.py:34
  230.9 54.0 %collective-permute-start.7 = (bf16[1,128,4096]{2,1,0:T(8,128)(2,1)}, bf16[1,128,4096]{2,1,0:T(8,128)(2,1)S(1)}, u32[]{:S(2)}, u32[]{:S(2)}) collective-permute-start(bf16[1,128,4096]{2,1,0:T(8,128)(2,1)} %copy.64), channel_id=1, source_target_pairs={{0,64},{64,128},{128,192},{192,256},{256,320},{320,384},{384,448},... | collective-permute-start | bytes 3145736 | tf_op jit(solution)/shard_map/ppermute | solution.py:34
  232.8 52.1 %collective-permute-start.8 = (bf16[1,128,4096]{2,1,0:T(8,128)(2,1)}, bf16[1,128,4096]{2,1,0:T(8,128)(2,1)S(1)}, u32[]{:S(2)}, u32[]{:S(2)}) collective-permute-start(bf16[1,128,4096]{2,1,0:T(8,128)(2,1)} %copy.65), channel_id=1, source_target_pairs={{64,0},{128,64},{192,128},{256,192},{320,256},{384,320},{448,384},... | collective-permute-start | bytes 3145736 | tf_op jit(solution)/shard_map/ppermute | solution.py:34
where the time goes:
time: 289 us; the launch traced here: 287 us
  waiting for transfers between devices  114 us (39%)
  starting transfers between devices  68 us (24%)
  local copies, waits for them, and re-layouts  56 us (19%)
  matrix products  28.2 us (10%)
  other arithmetic  11.8 us (4%)
  loops' own time  5.68 us (2%)
  between operations  3.56 us (1%)
    ppermute x12, waiting for transfers between devices, from_behind(): return lax.ppermute(value, axis, pairs)  75.8 us
    ppermute x12, starting transfers between devices, from_behind(): return lax.ppermute(value, axis, pairs)  57.3 us
    ppermute x1, waiting for transfers between devices, extended(): lax.ppermute(tail, axis, [(i, (i + 1) % count) for i in range(ends)])  25.9 us
    unnamed x24, local copies, waits for them, and re-layouts  13 us
    ppermute x1, waiting for transfers between devices, extended(): lax.ppermute(head, axis, [((i + 1) % count, i) for i in range(ends)])  12 us
    sub x4, matrix products, single_grouping(): weights = jnp.exp(scores - top)  8.13 us
    ppermute x1, starting transfers between devices, extended(): lax.ppermute(head, axis, [((i + 1) % count, i) for i in range(ends)])  7.61 us
    another operation x3, local copies, waits for them, and re-layouts, on_device(): partial_grads = jnp.stack([key_parts, value_parts])  6.14 us
  transfers between devices with their start and end apart: 14, of which 8 were waited for; matrix products, arithmetic and copies ran while one was open for 7% of the time, Pallas kernels for 0%

commit v1 on v0

v1 whole, which is shorter than its diff:
```python
import functools
import math

import jax
import jax.numpy as jnp
from jax import lax
from jax.experimental import pallas as pl
from jax.experimental.pallas import tpu as pltpu
from jax.sharding import PartitionSpec as P

QUERY_HEADS = 32
KEY_VALUE_HEADS = 4
HEAD_SIZE = 128
GROUP = QUERY_HEADS // KEY_VALUE_HEADS
MESH = pl.DeviceIdType.MESH
F32 = jnp.float32
BF16 = jnp.bfloat16
LOW = -1e30


def _nt(a, b):
    return lax.dot_general(a, b, (((1,), (1,)), ((), ())), preferred_element_type=F32)


def _nn(a, b):
    return lax.dot_general(a, b, (((1,), (0,)), ((), ())), preferred_element_type=F32)


def _tn(a, b):
    return lax.dot_general(a, b, (((0,), (0,)), ((), ())), preferred_element_type=F32)


def one_of(index, choices):
    first, second, third, fourth = choices
    return lax.select(
        index < 2, lax.select(index == 0, first, second), lax.select(index == 2, third, fourth)
    )


def _kernel(
    sizes,
    plan_ref,
    seg_ref,
    q_hbm,
    k_hbm,
    v_hbm,
    do_hbm,
    so_out,
    qg_out,
    kg_out,
    vg_out,
    kv,
    qb,
    dob,
    att,
    dqb,
    bias,
    parts,
    loc,
    ret,
    back,
    psend,
    precv,
    loc_sem,
    kv_send,
    kv_recv,
    q_send,
    q_recv,
    out_send,
    out_recv,
    ret_send,
    ret_recv,
    fin_send,
    fin_recv,
):
    n_pipe, n_ctx = sizes
    rows = k_hbm.shape[0]
    half = rows // 2
    width = GROUP * HEAD_SIZE
    window = 8 * half
    pad = 3 * half
    groups = KEY_VALUE_HEADS
    scale = 1.0 / math.sqrt(HEAD_SIZE)
    exp_scale = scale * math.log2(math.e)

    p = lax.axis_index("pipe")
    c = lax.axis_index("ctx")
    d = lax.axis_index("dp")
    me = 2 * c + d

    def at(dc, dd):
        return {"pipe": p, "ctx": lax.rem(c + dc + n_ctx, n_ctx), "dp": dd}

    other = at(0, 1 - d)
    across = at(2 * d - 1, 1 - d)
    above = at(d, 1 - d)
    below = at(d - 1, 1 - d)
    up1, up2, down1, down2 = at(1, d), at(2, d), at(-1, d), at(-2, d)
    later = {"pipe": lax.rem(p + 1, n_pipe), "ctx": c, "dp": d}
    earlier = {"pipe": lax.rem(p + n_pipe - 1, n_pipe), "ctx": c, "dp": d}

    def remote(src, dst, send, recv, target):
        return pltpu.make_async_remote_copy(
            src_ref=src, dst_ref=dst, send_sem=send, recv_sem=recv, device_id=target, device_id_type=MESH
        )

    own = pl.ds(4 * rows, rows)
    kv_width = k_hbm.shape[1]
    own_k = pltpu.make_async_copy(k_hbm, kv.at[own, pl.ds(0, kv_width)], loc_sem.at[0])
    own_v = pltpu.make_async_copy(v_hbm, kv.at[own, pl.ds(kv_width, kv_width)], loc_sem.at[1])

    def own_q(g):
        return pltpu.make_async_copy(
            q_hbm.at[:, pl.ds(pl.multiple_of(g * width, width), width)],
            qb.at[g, pl.ds(half, rows)],
            loc_sem.at[2 + g],
        )

    def own_do(g):
        return pltpu.make_async_copy(
            do_hbm.at[:, pl.ds(pl.multiple_of(g * width, width), width)], dob.at[g], loc_sem.at[2 + groups + g]
        )

    own_k.start()
    own_v.start()
    for g in range(groups):
        own_q(g).start()
    for g in range(groups):
        own_do(g).start()

    barrier = pltpu.get_barrier_semaphore()
    for target in (other, across, up1, up2, down1, down2):
        pl.semaphore_signal(barrier, inc=1, device_id=target, device_id_type=MESH)

    @pl.when(p < n_pipe - 1)
    def _():
        pl.semaphore_signal(barrier, inc=1, device_id=later, device_id_type=MESH)

    @pl.when(p > 0)
    def _():
        pl.semaphore_signal(barrier, inc=1, device_id=earlier, device_id_type=MESH)

    own_k.wait()
    own_v.wait()
    for g in range(groups):
        own_q(g).wait()
    pl.semaphore_wait(
        barrier, 6 + jnp.where(p < n_pipe - 1, 1, 0).astype(jnp.int32) + jnp.where(p > 0, 1, 0).astype(jnp.int32)
    )

    def kv_copy(kind, source, place, target):
        return remote(
            kv.at[pl.ds(pl.multiple_of(source * rows, rows), rows)],
            kv.at[pl.ds(pl.multiple_of(place * rows, rows), rows)],
            kv_send.at[kind],
            kv_recv.at[kind],
            target,
        )

    kv_other = kv_copy(0, 4, 3 + 2 * d, other)
    kv_up1 = kv_copy(1, 4, 2, up1)
    kv_up2 = kv_copy(2, 4, 0, up2)
    kv_pass1 = kv_copy(3, 5 - 2 * d, 3 - 2 * d, up1)
    kv_pass2 = kv_copy(4, 5 - 2 * d, 1 + 4 * d, at(2 - 3 * d, d))

    def q_below(g):
        return remote(
            qb.at[g, pl.ds(half, half)], qb.at[g, pl.ds(3 * half, half)], q_send.at[0, g], q_recv.at[0, g], below
        )

    def q_above(g):
        return remote(
            qb.at[g, pl.ds(2 * half, half)], qb.at[g, pl.ds(0, half)], q_send.at[1, g], q_recv.at[1, g], above
        )

    kv_other.start()
    kv_up1.start()
    kv_up2.start()
    for g in range(groups):
        q_below(g).start()
        q_above(g).start()

    zeros = jnp.zeros((pad, 2 * HEAD_SIZE), F32)
    shifts = []
    row_at = lax.broadcasted_iota(jnp.int32, seg_ref.shape, 0)
    for s in range(2):
        block = plan_ref[2 * me + s]
        shifts.append(block - 2 * me + 1)
        pair = lax.div(block, 2)
        line = jnp.sum(jnp.where(row_at == pair, seg_ref[...].astype(F32), 0.0), axis=0, keepdims=True)
        lane = lax.broadcasted_iota(jnp.int32, (half, rows), 1)
        sub = lax.broadcasted_iota(jnp.int32, (half, rows), 0)
        picked = jnp.where(lane == sub + (block - 2 * pair) * half, jnp.broadcast_to(line, (half, rows)), 0.0)
        mine = jnp.sum(picked, axis=1, keepdims=True)

        def count(r, total, mine=mine):
            row = seg_ref[pl.ds(r, 1), :].astype(F32)
            return total + jnp.where(row < mine, 1.0, 0.0)

        total = lax.fori_loop(0, seg_ref.shape[0], count, jnp.zeros((half, rows), F32))
        first = jnp.sum(total, axis=1, keepdims=True)
        key_at = lax.broadcasted_iota(jnp.int32, (half, window), 1) + (block - 7) * half
        query_at = lax.broadcasted_iota(jnp.int32, (half, window), 0) + block * half
        seen = (key_at.astype(F32) >= first) & (key_at <= query_at)
        bias[s] = jnp.where(seen, 0.0, LOW)
        parts[s, pl.ds(0, pad)] = zeros
        parts[s, pl.ds(pad + window, pad + rows - half)] = jnp.zeros((pad + rows - half, 2 * HEAD_SIZE), F32)

    kv_other.wait_recv()
    kv_pass1.start()
    kv_pass2.start()
    for copy in (kv_up1, kv_up2, kv_pass1, kv_pass2):
        copy.wait_recv()
    for g in range(groups):
        own_do(g).wait()

    def columns(g):
        return pl.ds(pl.multiple_of(g * width, width), width)

    def att_copy(g):
        return remote(att.at[g], so_out.at[:, columns(g)], out_send.at[0, g], out_recv.at[0, g], later)

    def dq_copy(g):
        return remote(dqb.at[g], qg_out.at[:, columns(g)], out_send.at[1, g], out_recv.at[1, g], earlier)

    def ret_copy(g, kind):
        source, target = ((0, down2), (2, down1), (3 - 2 * d, down1), (1 + 4 * d, at(3 * d - 2, d)))[kind]
        return remote(ret.at[g, source], back.at[g, kind], ret_send.at[g, kind], ret_recv.at[g, kind], target)

    def fin_copy(g):
        return remote(psend.at[g], precv.at[g], fin_send.at[g], fin_recv.at[g], other)

    def window_part(o):
        total = None
        for s in range(2):
            starts = [pl.multiple_of(pad - k * half + o * rows, half) for k in range(4)]
            one = one_of(shifts[s], [parts[s, pl.ds(start, rows), :] for start in starts])
            total = one if total is None else total + one
        return total

    def pass_on(g):
        for kind in range(4):
            ret_copy(g, kind).wait_recv()
        total = loc[g, 1] + back[g, 2].astype(F32) + back[g, 3].astype(F32)
        psend[g] = total.astype(BF16)
        fin_copy(g).start()

    def one_group(g, carry):
        q_below(g).wait_recv()
        q_above(g).wait_recv()
        for s in range(2):
            shift = shifts[s]
            chosen = one_of(shift, [qb[g, pl.ds(k * half, half), :] for k in range(4)])
            grad = dob[g, pl.ds(s * half, half), :]
            heads = [slice(h * HEAD_SIZE, (h + 1) * HEAD_SIZE) for h in range(GROUP)]
            qs = jnp.concatenate([chosen[:, h] for h in heads], axis=0)
            gs = jnp.concatenate([grad[:, h] for h in heads], axis=0)
            k_place = pl.ds(pl.multiple_of(g * HEAD_SIZE, HEAD_SIZE), HEAD_SIZE)
            v_place = pl.ds(pl.multiple_of(kv_width + g * HEAD_SIZE, HEAD_SIZE), HEAD_SIZE)
            ks = one_of(shift, [kv[pl.ds(k * half, window), k_place] for k in range(4)])
            vs = one_of(shift, [kv[pl.ds(k * half, window), v_place] for k in range(4)])
            scores = _nt(qs, ks).reshape(GROUP, half, window) + bias[s][None]
            scores = scores.reshape(GROUP * half, window)
            top = jnp.max(scores, axis=1, keepdims=True)
            weights = jnp.exp2((scores - top) * exp_scale)
            probs = weights * (1.0 / jnp.sum(weights, axis=1, keepdims=True))
            low = probs.astype(BF16)
            attended = _nn(low, vs).astype(BF16)
            grad_probs = _nt(gs, vs)
            delta = jnp.sum(gs.astype(F32) * attended.astype(F32), axis=1, keepdims=True)
            grad_scores = (probs * (grad_probs - delta)).astype(BF16)
            query_grad = (_nn(grad_scores, ks) * scale).astype(BF16)
            for h in range(GROUP):
                att[g, pl.ds(s * half, half), heads[h]] = attended[h * half : (h + 1) * half]
                dqb[g, pl.ds(s * half, half), heads[h]] = query_grad[h * half : (h + 1) * half]
            parts[s, pl.ds(pad, window), pl.ds(0, HEAD_SIZE)] = _tn(grad_scores, qs) * scale
            parts[s, pl.ds(pad, window), pl.ds(HEAD_SIZE, HEAD_SIZE)] = _tn(low, gs)
        for o in range(6):
            ret[g, o] = window_part(o).astype(BF16)
        loc[g, 0] = window_part(4)
        loc[g, 1] = window_part(5 - 2 * d)
        for kind in range(4):
            ret_copy(g, kind).start()

        @pl.when(p < n_pipe - 1)
        def _():
            att_copy(g).start()

        @pl.when(p > 0)
        def _():
            dq_copy(g).start()

        @pl.when(g > 0)
        def _():
            pass_on(g - 1)

        return carry

    lax.fori_loop(0, groups, one_group, 0)
    pass_on(groups - 1)

    def finish(g, carry):
        fin_copy(g).wait_recv()
        total = loc[g, 0] + back[g, 0].astype(F32) + back[g, 1].astype(F32) + precv[g].astype(F32)
        place = pl.ds(pl.multiple_of(g * HEAD_SIZE, HEAD_SIZE), HEAD_SIZE)
        kg_out[:, place] = total[:, :HEAD_SIZE].astype(BF16)
        vg_out[:, place] = total[:, HEAD_SIZE:].astype(BF16)
        return carry

    lax.fori_loop(0, groups, finish, 0)

    for copy in (kv_other, kv_up1, kv_up2, kv_pass1, kv_pass2):
        copy.wait_send()

    def drain(g, carry):
        q_below(g).wait_send()
        q_above(g).wait_send()
        for kind in range(4):
            ret_copy(g, kind).wait_send()
        fin_copy(g).wait_send()

        @pl.when(p < n_pipe - 1)
        def _():
            att_copy(g).wait_send()
            dq_copy(g).wait_recv()

        @pl.when(p > 0)
        def _():
            dq_copy(g).wait_send()
            att_copy(g).wait_recv()

        return carry

    lax.fori_loop(0, groups, drain, 0)


def _on_device(sizes, section_queries, section_keys, cascade_value_rows, output_grad, segments, stretch_plan):
    _, rows, width = section_queries.shape
    kv_width = section_keys.shape[2]
    groups, half = KEY_VALUE_HEADS, rows // 2
    share = width // groups
    hbm = pl.BlockSpec(memory_space=pl.ANY)
    vmem = pl.BlockSpec(memory_space=pltpu.VMEM)
    dma = pltpu.SemaphoreType.DMA
    attended, query_grad, key_grad, value_grad = pl.pallas_call(
        functools.partial(_kernel, sizes),
        out_shape=[
            jax.ShapeDtypeStruct((rows, width), BF16),
            jax.ShapeDtypeStruct((rows, width), BF16),
            jax.ShapeDtypeStruct((rows, kv_width), BF16),
            jax.ShapeDtypeStruct((rows, kv_width), BF16),
        ],
        in_specs=[pl.BlockSpec(memory_space=pltpu.SMEM), vmem, hbm, hbm, hbm, hbm],
        out_specs=[hbm, hbm, vmem, vmem],
        scratch_shapes=[
            pltpu.VMEM((6 * rows, 2 * kv_width), BF16),
            pltpu.VMEM((groups, 2 * rows, share), BF16),
            pltpu.VMEM((groups, rows, share), BF16),
            pltpu.VMEM((groups, rows, share), BF16),
            pltpu.VMEM((groups, rows, share), BF16),
            pltpu.VMEM((2, half, 8 * half), F32),
            pltpu.VMEM((2, 14 * half + rows // 2, 2 * HEAD_SIZE), F32),
            pltpu.VMEM((groups, 2, rows, 2 * HEAD_SIZE), F32),
            pltpu.VMEM((groups, 6, rows, 2 * HEAD_SIZE), BF16),
            pltpu.VMEM((groups, 4, rows, 2 * HEAD_SIZE), BF16),
            pltpu.VMEM((groups, rows, 2 * HEAD_SIZE), BF16),
            pltpu.VMEM((groups, rows, 2 * HEAD_SIZE), BF16),
            dma((2 + 2 * groups,)),
            dma((5,)),
            dma((5,)),
            dma((2, groups)),
            dma((2, groups)),
            dma((2, groups)),
            dma((2, groups)),
            dma((groups, 4)),
            dma((groups, 4)),
            dma((groups,)),
            dma((groups,)),
        ],
        compiler_params=pltpu.CompilerParams(
            collective_id=0, has_side_effects=True, vmem_limit_bytes=48 * 1024 * 1024
        ),
    )(
        stretch_plan,
        segments.reshape(-1, rows),
        section_queries[0],
        section_keys[0],
        cascade_value_rows[0],
        output_grad[0],
    )
    place = lax.axis_index("pipe")
    section_output = jnp.where(place == 0, jnp.zeros_like(attended), attended)
    query_grad_sent = jnp.where(place == sizes[0] - 1, jnp.zeros_like(query_grad), query_grad)
    return section_output[None], query_grad_sent[None], key_grad[None], value_grad[None]


def solution(mesh):
    spread = P("pipe", ("ctx", "dp"), None)
    return jax.shard_map(
        functools.partial(_on_device, (mesh.shape["pipe"], mesh.shape["ctx"])),
        mesh=mesh,
        in_specs=(spread, spread, spread, spread, P(), P()),
        out_specs=(spread, spread, spread, spread),
        check_vma=False,
    )
```

time: 289 us -> 118 us (0.41)
  the two profiles are of different devices: /device:TPU:94 before, /device:TPU:1 now
where the time goes in v1:
time: 118 us; the launch traced here: 116 us
  Pallas kernels  107 us (91%)
  local copies, waits for them, and re-layouts  6.97 us (6%)
  other arithmetic  1.46 us (1%)
    pallas_call x1, Pallas kernels, _on_device(): pl.pallas_call(functools.partial(_kernel, sizes), out_shape=[jax.ShapeDty...  107 us
    unnamed x14, local copies, waits for them, and re-layouts  6.97 us

profile of v1, /device:TPU:1, one launch (start us, length us, event | category | flops | bytes accessed | tf_op | source)
XLA Modules:
  0.0 116.5 jit_solution(6041360643821520565)
XLA Ops:
  0.6 0.0 copy-start.5
  0.7 0.6 copy-done.5
  1.3 0.0 copy-start
  1.3 1.2 %copy-done = bf16[1,128,4096]{2,1,0:T(8,128)(2,1)S(1)} copy-done((bf16[1,128,4096]{2,1,0:T(8,128)(2,1)S(1)}, bf16[1,128,4096]{2,1,0:T(8,128)(2,1)}, u32[]{:S(2)}) %copy-start) | copy-done | bytes 1048600
  2.5 0.0 copy-start.1
  2.5 1.2 %copy-done.1 = bf16[1,128,4096]{2,1,0:T(8,128)(2,1)S(1)} copy-done((bf16[1,128,4096]{2,1,0:T(8,128)(2,1)S(1)}, bf16[1,128,4096]{2,1,0:T(8,128)(2,1)}, u32[]{:S(2)}) %copy-start.1) | copy-done | bytes 1048600
  3.7 0.0 copy-start.2
  3.8 0.9 copy-done.2
  4.7 0.0 copy-start.3
  4.7 0.9 copy-done.3
  5.6 0.0 copy-start.4
  5.6 0.8 copy-done.4
  6.3 107.4 %shard_map.93 = (bf16[128,4096]{1,0:T(8,128)(2,1)S(1)}, bf16[128,4096]{1,0:T(8,128)(2,1)S(1)}, bf16[128,512]{1,0:T(8,128)(2,1)S(1)}, bf16[128,512]{1,0:T(8,128)(2,1)S(1)}) custom-call(s32[128]{0:T(128)S(1)} %copy-done.5, s32[64,128]{1,0:T(8,128)S(1)} %bitcast.17, bf16[128,4096]{1,0:T(8,128)(2,1)S(1)} %bitcast.11, bf16[128,512]{1,0:T(8,128)(2,1)S(1)} %bitcast.15, ...), custom_call_target="tpu_custom_call" | custom-call | tf_op jit(solution)/shard_map/pallas_call | solution.py:345
  113.7 1.5 %select_bitcast_fusion = (bf16[1,128,4096]{2,1,0:T(8,128)(2,1)}, bf16[1,128,4096]{2,1,0:T(8,128)(2,1)}) fusion(bf16[128,4096]{1,0:T(8,128)(2,1)S(1)} %get-tuple-element.9, pred[]{:T(512)S(6)} %eq.7, bf16[128,4096]{1,0:T(8,128)(2,1)S(1)} %get-tuple-element.8, pred[]{:T(512)S(6)} %eq.6), kind=kLoop, calls=%fused_computation | loop fusion | flops 1048576 | bytes 4194306 | tf_op jit(solution)/shard_map/broadcast_in_dim | solution.py:394
  115.2 0.7 copy.12
  115.8 0.7 copy.13
Async XLA Ops:
  0.6 0.7 copy-start.5
  1.3 1.2 %copy-start = (bf16[1,128,4096]{2,1,0:T(8,128)(2,1)S(1)}, bf16[1,128,4096]{2,1,0:T(8,128)(2,1)}, u32[]{:S(2)}) copy-start(bf16[1,128,4096]{2,1,0:T(8,128)(2,1)} %param.6) | copy-start | bytes 3145732
  2.5 1.2 %copy-start.1 = (bf16[1,128,4096]{2,1,0:T(8,128)(2,1)S(1)}, bf16[1,128,4096]{2,1,0:T(8,128)(2,1)}, u32[]{:S(2)}) copy-start(bf16[1,128,4096]{2,1,0:T(8,128)(2,1)} %param.9) | copy-start | bytes 3145732
  3.7 0.9 copy-start.2
  4.7 0.9 copy-start.3
  5.6 0.8 copy-start.4

commit v2 on v1

--- a/solution.py
+++ b/solution.py
@@ -72,6 +72,7 @@
     ret_recv,
     fin_send,
     fin_recv,
+    hello,
 ):
     n_pipe, n_ctx = sizes
     rows = k_hbm.shape[0]
@@ -93,8 +94,6 @@
 
     other = at(0, 1 - d)
     across = at(2 * d - 1, 1 - d)
-    above = at(d, 1 - d)
-    below = at(d - 1, 1 - d)
     up1, up2, down1, down2 = at(1, d), at(2, d), at(-1, d), at(-2, d)
     later = {"pipe": lax.rem(p + 1, n_pipe), "ctx": c, "dp": d}
     earlier = {"pipe": lax.rem(p + n_pipe - 1, n_pipe), "ctx": c, "dp": d}
@@ -129,24 +128,38 @@
         own_do(g).start()
 
     barrier = pltpu.get_barrier_semaphore()
-    for target in (other, across, up1, up2, down1, down2):
-        pl.semaphore_signal(barrier, inc=1, device_id=target, device_id_type=MESH)
-
-    @pl.when(p < n_pipe - 1)
+    not_first, not_last = p > 0, p < n_pipe - 1
+
+    def signal(semaphore, target):
+        pl.semaphore_signal(semaphore, inc=1, device_id=target, device_id_type=MESH)
+
+    for target in (other, down1, down2):
+        signal(barrier, target)
+
+    @pl.when(d == 0)
     def _():
-        pl.semaphore_signal(barrier, inc=1, device_id=later, device_id_type=MESH)
-
-    @pl.when(p > 0)
+        signal(barrier, across)
+
+    @pl.when(not_last)
     def _():
-        pl.semaphore_signal(barrier, inc=1, device_id=earlier, device_id_type=MESH)
+        signal(barrier, later)
+
+    @pl.when(not_first)
+    def _():
+        signal(barrier, earlier)
 
     own_k.wait()
     own_v.wait()
     for g in range(groups):
         own_q(g).wait()
-    pl.semaphore_wait(
-        barrier, 6 + jnp.where(p < n_pipe - 1, 1, 0).astype(jnp.int32) + jnp.where(p > 0, 1, 0).astype(jnp.int32)
-    )
+    pl.semaphore_wait(barrier, 3 + d + not_last.astype(jnp.int32) + not_first.astype(jnp.int32))
+    signal(hello.at[0], up1)
+    signal(hello.at[1], up2)
+
+    @pl.when(d == 1)
+    def _():
+        signal(hello.at[2], across)
+
 
     def kv_copy(kind, source, place, target):
         return remote(
@@ -163,22 +176,31 @@
     kv_pass1 = kv_copy(3, 5 - 2 * d, 3 - 2 * d, up1)
     kv_pass2 = kv_copy(4, 5 - 2 * d, 1 + 4 * d, at(2 - 3 * d, d))
 
-    def q_below(g):
+    def q_other(g):
+        first, place = half * (2 - d), 3 * half * d
         return remote(
-            qb.at[g, pl.ds(half, half)], qb.at[g, pl.ds(3 * half, half)], q_send.at[0, g], q_recv.at[0, g], below
-        )
-
-    def q_above(g):
+            qb.at[g, pl.ds(pl.multiple_of(first, half), half)],
+            qb.at[g, pl.ds(pl.multiple_of(place, half), half)],
+            q_send.at[0, g],
+            q_recv.at[0, g],
+            other,
+        )
+
+    def q_across(g):
+        first, place = half * (1 + d), 3 * half * (1 - d)
         return remote(
-            qb.at[g, pl.ds(2 * half, half)], qb.at[g, pl.ds(0, half)], q_send.at[1, g], q_recv.at[1, g], above
+            qb.at[g, pl.ds(pl.multiple_of(first, half), half)],
+            qb.at[g, pl.ds(pl.multiple_of(place, half), half)],
+            q_send.at[1, g],
+            q_recv.at[1, g],
+            across,
         )
 
     kv_other.start()
     kv_up1.start()
     kv_up2.start()
-    for g in range(groups):
-        q_below(g).start()
-        q_above(g).start()
+    q_other(0).start()
+    q_other(1).start()
 
     zeros = jnp.zeros((pad, 2 * HEAD_SIZE), F32)
     shifts = []
@@ -206,6 +228,18 @@
         parts[s, pl.ds(0, pad)] = zeros
         parts[s, pl.ds(pad + window, pad + rows - half)] = jnp.zeros((pad + rows - half, 2 * HEAD_SIZE), F32)
 
+    @pl.when(d == 0)
+    def _():
+        pl.semaphore_wait(hello.at[2], 1)
+
+    q_across(0).start()
+    q_across(1).start()
+    for g in range(2, groups):
+        q_other(g).start()
+        q_across(g).start()
+    pl.semaphore_wait(hello.at[0], 1)
+    pl.semaphore_wait(hello.at[1], 1)
+
     kv_other.wait_recv()
     kv_pass1.start()
     kv_pass2.start()
@@ -246,8 +280,8 @@
         fin_copy(g).start()
 
     def one_group(g, carry):
-        q_below(g).wait_recv()
-        q_above(g).wait_recv()
+        q_other(g).wait_recv()
+        q_across(g).wait_recv()
         for s in range(2):
             shift = shifts[s]
             chosen = one_of(shift, [qb[g, pl.ds(k * half, half), :] for k in range(4)])
@@ -282,11 +316,11 @@
         for kind in range(4):
             ret_copy(g, kind).start()
 
-        @pl.when(p < n_pipe - 1)
+        @pl.when(not_last)
         def _():
             att_copy(g).start()
 
-        @pl.when(p > 0)
+        @pl.when(not_first)
         def _():
             dq_copy(g).start()
 
@@ -313,18 +347,18 @@
         copy.wait_send()
 
     def drain(g, carry):
-        q_below(g).wait_send()
-        q_above(g).wait_send()
+        q_other(g).wait_send()
+        q_across(g).wait_send()
         for kind in range(4):
             ret_copy(g, kind).wait_send()
         fin_copy(g).wait_send()
 
-        @pl.when(p < n_pipe - 1)
+        @pl.when(not_last)
         def _():
             att_copy(g).wait_send()
             dq_copy(g).wait_recv()
 
-        @pl.when(p > 0)
+        @pl.when(not_first)
         def _():
             dq_copy(g).wait_send()
             att_copy(g).wait_recv()
@@ -339,7 +373,7 @@
     kv_width = section_keys.shape[2]
     groups, half = KEY_VALUE_HEADS, rows // 2
     share = width // groups
-    hbm = pl.BlockSpec(memory_space=pl.ANY)
+    hbm = pl.BlockSpec(memory_space=pltpu.HBM)
     vmem = pl.BlockSpec(memory_space=pltpu.VMEM)
     dma = pltpu.SemaphoreType.DMA
     attended, query_grad, key_grad, value_grad = pl.pallas_call(
@@ -376,9 +410,10 @@
             dma((groups, 4)),
             dma((groups,)),
             dma((groups,)),
+            pltpu.SemaphoreType.REGULAR((3,)),
         ],
         compiler_params=pltpu.CompilerParams(
-            collective_id=0, has_side_effects=True, vmem_limit_bytes=48 * 1024 * 1024
+            collective_id=0, has_side_effects=True, vmem_limit_bytes=56 * 1024 * 1024
         ),
     )(
         stretch_plan,

time: 118 us -> 103 us (0.87)
  Pallas kernels: 107 us -> 97 us
  local copies, waits for them, and re-layouts: 6.97 us -> 1.61 us
  other arithmetic: 1.46 us -> 3.04 us
    pallas_call x1, Pallas kernels: 107 us -> 97 us  [_on_device(): pl.pallas_call(functools.partial(_kernel, sizes), out_shape=[jax.ShapeDty...]
    unnamed x14 -> x6, local copies, waits for them, and re-layouts: 6.97 us -> 1.61 us
    broadcast_in_dim x1, other arithmetic: 1.46 us -> 3.04 us  [_on_device(): query_grad_sent[None]]
where the time goes in v2:
time: 103 us; the launch traced here: 102 us
  Pallas kernels  97 us (94%)
  other arithmetic  3.04 us (3%)
  local copies, waits for them, and re-layouts  1.61 us (2%)
    pallas_call x1, Pallas kernels, _on_device(): pl.pallas_call(functools.partial(_kernel, sizes), out_shape=[jax.ShapeDty...  97 us
    broadcast_in_dim x1, other arithmetic, _on_device(): query_grad_sent[None]  3.04 us

profile of v2, /device:TPU:1, one launch (start us, length us, event | category | flops | bytes accessed | tf_op | source)
XLA Modules:
  0.0 102.3 jit_solution(7347879160432990786)
XLA Ops:
  0.6 97.0 %shard_map.93 = (bf16[128,4096]{1,0:T(8,128)(2,1)}, bf16[128,4096]{1,0:T(8,128)(2,1)}, bf16[128,512]{1,0:T(8,128)(2,1)}, bf16[128,512]{1,0:T(8,128)(2,1)}) custom-call(s32[128]{0:T(128)} %plan_ref.1, s32[64,128]{1,0:T(8,128)} %bitcast.17, bf16[128,4096]{1,0:T(8,128)(2,1)} %bitcast.11, bf16[128,512]{1,0:T(8,128)(2,1)} %bitcast.15, bf16[128,512]{1,0:T(8,128)(2,1)} %bitcast.16, ...), custom_call_target="tpu_custom_call" | custom-call | tf_op jit(solution)/shard_map/pallas_call | solution.py:379
  97.7 0.0 copy-start.1
  97.7 3.0 %select_bitcast_fusion = (bf16[1,128,4096]{2,1,0:T(8,128)(2,1)}, bf16[1,128,4096]{2,1,0:T(8,128)(2,1)}) fusion(bf16[128,4096]{1,0:T(8,128)(2,1)} %get-tuple-element.9, pred[]{:T(512)S(6)} %eq.7, bf16[128,4096]{1,0:T(8,128)(2,1)} %get-tuple-element.8, pred[]{:T(512)S(6)} %eq.6), kind=kLoop, calls=%fused_computation | loop fusion | flops 1048576 | bytes 4194306 | tf_op jit(solution)/shard_map/broadcast_in_dim | solution.py:429
  100.7 0.0 copy-done.1
  100.7 0.0 copy-start
  100.7 0.7 copy.12
  101.4 0.3 copy-done
  101.7 0.7 copy.13
Async XLA Ops:
  97.7 3.1 %copy-start.1 = (bf16[128,512]{1,0:T(8,128)(2,1)S(1)}, bf16[128,512]{1,0:T(8,128)(2,1)}, u32[]{:S(2)}) copy-start(bf16[128,512]{1,0:T(8,128)(2,1)} %get-tuple-element.10) | copy-start | bytes 393220
  100.7 1.0 copy-start

commit v3 on v2

--- a/solution.py
+++ b/solution.py
@@ -16,6 +16,7 @@
 F32 = jnp.float32
 BF16 = jnp.bfloat16
 LOW = -1e30
+PIECES = 4
 
 
 def _nt(a, b):
@@ -104,24 +105,29 @@
         )
 
     own = pl.ds(4 * rows, rows)
-    kv_width = k_hbm.shape[1]
-    own_k = pltpu.make_async_copy(k_hbm, kv.at[own, pl.ds(0, kv_width)], loc_sem.at[0])
-    own_v = pltpu.make_async_copy(v_hbm, kv.at[own, pl.ds(kv_width, kv_width)], loc_sem.at[1])
+
+    def own_kv(g):
+        part = pl.ds(pl.multiple_of(g * HEAD_SIZE, HEAD_SIZE), HEAD_SIZE)
+        return (
+            pltpu.make_async_copy(k_hbm.at[:, part], kv.at[g, own, pl.ds(0, HEAD_SIZE)], loc_sem.at[0, g]),
+            pltpu.make_async_copy(v_hbm.at[:, part], kv.at[g, own, pl.ds(HEAD_SIZE, HEAD_SIZE)], loc_sem.at[1, g]),
+        )
 
     def own_q(g):
         return pltpu.make_async_copy(
             q_hbm.at[:, pl.ds(pl.multiple_of(g * width, width), width)],
             qb.at[g, pl.ds(half, rows)],
-            loc_sem.at[2 + g],
+            loc_sem.at[2, g],
         )
 
     def own_do(g):
         return pltpu.make_async_copy(
-            do_hbm.at[:, pl.ds(pl.multiple_of(g * width, width), width)], dob.at[g], loc_sem.at[2 + groups + g]
-        )
-
-    own_k.start()
-    own_v.start()
+            do_hbm.at[:, pl.ds(pl.multiple_of(g * width, width), width)], dob.at[g], loc_sem.at[3, g]
+        )
+
+    for g in range(groups):
+        for copy in own_kv(g):
+            copy.start()
     for g in range(groups):
         own_q(g).start()
     for g in range(groups):
@@ -148,9 +154,9 @@
     def _():
         signal(barrier, earlier)
 
-    own_k.wait()
-    own_v.wait()
     for g in range(groups):
+        for copy in own_kv(g):
+            copy.wait()
         own_q(g).wait()
     pl.semaphore_wait(barrier, 3 + d + not_last.astype(jnp.int32) + not_first.astype(jnp.int32))
     signal(hello.at[0], up1)
@@ -161,20 +167,21 @@
         signal(hello.at[2], across)
 
 
-    def kv_copy(kind, source, place, target):
+    def kv_copy(kind, g):
+        source, place, target = (
+            (4, 3 + 2 * d, other),
+            (4, 2, up1),
+            (4, 0, up2),
+            (5 - 2 * d, 3 - 2 * d, up1),
+            (5 - 2 * d, 1 + 4 * d, at(2 - 3 * d, d)),
+        )[kind]
         return remote(
-            kv.at[pl.ds(pl.multiple_of(source * rows, rows), rows)],
-            kv.at[pl.ds(pl.multiple_of(place * rows, rows), rows)],
-            kv_send.at[kind],
-            kv_recv.at[kind],
+            kv.at[g, pl.ds(pl.multiple_of(source * rows, rows), rows)],
+            kv.at[g, pl.ds(pl.multiple_of(place * rows, rows), rows)],
+            kv_send.at[kind, g],
+            kv_recv.at[kind, g],
             target,
         )
-
-    kv_other = kv_copy(0, 4, 3 + 2 * d, other)
-    kv_up1 = kv_copy(1, 4, 2, up1)
-    kv_up2 = kv_copy(2, 4, 0, up2)
-    kv_pass1 = kv_copy(3, 5 - 2 * d, 3 - 2 * d, up1)
-    kv_pass2 = kv_copy(4, 5 - 2 * d, 1 + 4 * d, at(2 - 3 * d, d))
 
     def q_other(g):
         first, place = half * (2 - d), 3 * half * d
@@ -196,11 +203,12 @@
             across,
         )
 
-    kv_other.start()
-    kv_up1.start()
-    kv_up2.start()
+    for g in range(groups):
+        kv_copy(0, g).start()
+    kv_copy(1, 0).start()
+    kv_copy(2, 0).start()
+
     q_other(0).start()
-    q_other(1).start()
 
     zeros = jnp.zeros((pad, 2 * HEAD_SIZE), F32)
     shifts = []
@@ -233,18 +241,25 @@
         pl.semaphore_wait(hello.at[2], 1)
 
     q_across(0).start()
-    q_across(1).start()
-    for g in range(2, groups):
+    for g in range(1, groups):
         q_other(g).start()
         q_across(g).start()
     pl.semaphore_wait(hello.at[0], 1)
     pl.semaphore_wait(hello.at[1], 1)
 
-    kv_other.wait_recv()
-    kv_pass1.start()
-    kv_pass2.start()
-    for copy in (kv_up1, kv_up2, kv_pass1, kv_pass2):
-        copy.wait_recv()
+    def relay(g, carry):
+        kv_copy(0, g).wait_recv()
+        kv_copy(3, g).start()
+        kv_copy(4, g).start()
+
+        @pl.when(g + 1 < groups)
+        def _():
+            kv_copy(1, g + 1).start()
+            kv_copy(2, g + 1).start()
+
+        return carry
+
+    lax.fori_loop(0, groups, relay, 0)
     for g in range(groups):
         own_do(g).wait()
 
@@ -280,6 +295,8 @@
         fin_copy(g).start()
 
     def one_group(g, carry):
+        for kind in range(1, 5):
+            kv_copy(kind, g).wait_recv()
         q_other(g).wait_recv()
         q_across(g).wait_recv()
         for s in range(2):
@@ -289,10 +306,8 @@
             heads = [slice(h * HEAD_SIZE, (h + 1) * HEAD_SIZE) for h in range(GROUP)]
             qs = jnp.concatenate([chosen[:, h] for h in heads], axis=0)
             gs = jnp.concatenate([grad[:, h] for h in heads], axis=0)
-            k_place = pl.ds(pl.multiple_of(g * HEAD_SIZE, HEAD_SIZE), HEAD_SIZE)
-            v_place = pl.ds(pl.multiple_of(kv_width + g * HEAD_SIZE, HEAD_SIZE), HEAD_SIZE)
-            ks = one_of(shift, [kv[pl.ds(k * half, window), k_place] for k in range(4)])
-            vs = one_of(shift, [kv[pl.ds(k * half, window), v_place] for k in range(4)])
+            ks = one_of(shift, [kv[g, pl.ds(k * half, window), pl.ds(0, HEAD_SIZE)] for k in range(4)])
+            vs = one_of(shift, [kv[g, pl.ds(k * half, window), pl.ds(HEAD_SIZE, HEAD_SIZE)] for k in range(4)])
             scores = _nt(qs, ks).reshape(GROUP, half, window) + bias[s][None]
             scores = scores.reshape(GROUP * half, window)
             top = jnp.max(scores, axis=1, keepdims=True)
@@ -343,10 +358,9 @@
 
     lax.fori_loop(0, groups, finish, 0)
 
-    for copy in (kv_other, kv_up1, kv_up2, kv_pass1, kv_pass2):
-        copy.wait_send()
-
     def drain(g, carry):
+        for kind in range(5):
+            kv_copy(kind, g).wait_send()
         q_other(g).wait_send()
         q_across(g).wait_send()
         for kind in range(4):
@@ -366,6 +380,42 @@
         return carry
 
     lax.fori_loop(0, groups, drain, 0)
+
+
+def _place(sizes, so_in, qg_in, kg_in, vg_in, so_out, qg_out, kg_out, vg_out, so, qg, kg, vg, in_sem, out_sem):
+    p = lax.axis_index("pipe")
+    moves = []
+    for source, buffer, to, none in (
+        (so_in, so, so_out, 0),
+        (qg_in, qg, qg_out, sizes[0] - 1),
+        (kg_in, kg, kg_out, None),
+        (vg_in, vg, vg_out, None),
+    ):
+        pieces = 1 if none is None else PIECES
+        step = source.shape[0] // pieces
+        for k in range(pieces):
+            part, n = pl.ds(k * step, step), len(moves)
+            moves.append(
+                (
+                    pltpu.make_async_copy(source.at[part], buffer.at[part], in_sem.at[n]),
+                    pltpu.make_async_copy(buffer.at[part], to.at[part], out_sem.at[n]),
+                    none,
+                    buffer.at[part],
+                )
+            )
+    for load, _, _, _ in moves:
+        load.start()
+    for load, store, none, buffer in moves:
+        load.wait()
+        if none is not None:
+
+            @pl.when(p == none)
+            def _(buffer=buffer):
+                buffer[...] = jnp.zeros(buffer.shape, buffer.dtype)
+
+        store.start()
+    for _, store, _, _ in moves:
+        store.wait()
 
 
 def _on_device(sizes, section_queries, section_keys, cascade_value_rows, output_grad, segments, stretch_plan):
@@ -387,7 +437,7 @@
         in_specs=[pl.BlockSpec(memory_space=pltpu.SMEM), vmem, hbm, hbm, hbm, hbm],
         out_specs=[hbm, hbm, vmem, vmem],
         scratch_shapes=[
-            pltpu.VMEM((6 * rows, 2 * kv_width), BF16),
+            pltpu.VMEM((groups, 6 * rows, 2 * HEAD_SIZE), BF16),
             pltpu.VMEM((groups, 2 * rows, share), BF16),
             pltpu.VMEM((groups, rows, share), BF16),
             pltpu.VMEM((groups, rows, share), BF16),
@@ -399,9 +449,9 @@
             pltpu.VMEM((groups, 4, rows, 2 * HEAD_SIZE), BF16),
             pltpu.VMEM((groups, rows, 2 * HEAD_SIZE), BF16),
             pltpu.VMEM((groups, rows, 2 * HEAD_SIZE), BF16),
-            dma((2 + 2 * groups,)),
-            dma((5,)),
-            dma((5,)),
+            dma((4, groups)),
+            dma((5, groups)),
+            dma((5, groups)),
             dma((2, groups)),
             dma((2, groups)),
             dma((2, groups)),
@@ -423,9 +473,26 @@
         cascade_value_rows[0],
         output_grad[0],
     )
-    place = lax.axis_index("pipe")
-    section_output = jnp.where(place == 0, jnp.zeros_like(attended), attended)
-    query_grad_sent = jnp.where(place == sizes[0] - 1, jnp.zeros_like(query_grad), query_grad)
+    section_output, query_grad_sent, key_grad, value_grad = pl.pallas_call(
+        functools.partial(_place, sizes),
+        out_shape=[
+            jax.ShapeDtypeStruct((rows, width), BF16),
+            jax.ShapeDtypeStruct((rows, width), BF16),
+            jax.ShapeDtypeStruct((rows, kv_width), BF16),
+            jax.ShapeDtypeStruct((rows, kv_width), BF16),
+        ],
+        in_specs=[hbm] * 4,
+        out_specs=[hbm] * 4,
+        scratch_shapes=[
+            pltpu.VMEM((rows, width), BF16),
+            pltpu.VMEM((rows, width), BF16),
+            pltpu.VMEM((rows, kv_width), BF16),
+            pltpu.VMEM((rows, kv_width), BF16),
+            dma((2 * PIECES + 2,)),
+            dma((2 * PIECES + 2,)),
+        ],
+        compiler_params=pltpu.CompilerParams(vmem_limit_bytes=56 * 1024 * 1024),
+    )(attended, query_grad, key_grad, value_grad)
     return section_output[None], query_grad_sent[None], key_grad[None], value_grad[None]
 
 

time: 103 us -> 97.6 us (0.948)
  other arithmetic: 3.04 us -> 0 us
  local copies, waits for them, and re-layouts: 1.61 us -> 0 us
    pallas_call x1, Pallas kernels: 97 us -> 93.9 us  [_on_device(): pl.pallas_call(functools.partial(_kernel, sizes), out_shape=[jax.ShapeDty...]
    broadcast_in_dim x1 -> x0, other arithmetic: 3.04 us -> none  [_on_device(): query_grad_sent[None]]
    pallas_call x0 -> x1, Pallas kernels: none -> 2.51 us  [_on_device(): pl.pallas_call(functools.partial(_place, sizes), out_shape=[jax.ShapeDtyp...]
    unnamed x6 -> x0, local copies, waits for them, and re-layouts: 1.61 us -> none
where the time goes in v3:
time: 97.6 us; the launch traced here: 97 us
  Pallas kernels  96.4 us (99%)
    pallas_call x1, Pallas kernels, _on_device(): pl.pallas_call(functools.partial(_kernel, sizes), out_shape=[jax.ShapeDty...  93.9 us
    pallas_call x1, Pallas kernels, _on_device(): pl.pallas_call(functools.partial(_place, sizes), out_shape=[jax.ShapeDtyp...  2.51 us

profile of v3, /device:TPU:1, one launch (start us, length us, event | category | flops | bytes accessed | tf_op | source)
XLA Modules:
  0.0 97.0 jit_solution(8397956788434294082)
XLA Ops:
  0.6 93.9 %shard_map.93 = (bf16[128,4096]{1,0:T(8,128)(2,1)}, bf16[128,4096]{1,0:T(8,128)(2,1)}, bf16[128,512]{1,0:T(8,128)(2,1)}, bf16[128,512]{1,0:T(8,128)(2,1)}) custom-call(s32[128]{0:T(128)} %plan_ref.1, s32[64,128]{1,0:T(8,128)} %bitcast.13, bf16[128,4096]{1,0:T(8,128)(2,1)} %bitcast.9, bf16[128,512]{1,0:T(8,128)(2,1)} %bitcast.11, bf16[128,512]{1,0:T(8,128)(2,1)} %bitcast.12, ...), custom_call_target="tpu_custom_call" | custom-call | tf_op jit(solution)/shard_map/pallas_call | solution.py:429
  94.5 2.5 %shard_map.94 = (bf16[128,4096]{1,0:T(8,128)(2,1)}, bf16[128,4096]{1,0:T(8,128)(2,1)}, bf16[128,512]{1,0:T(8,128)(2,1)}, bf16[128,512]{1,0:T(8,128)(2,1)}) custom-call(bf16[128,4096]{1,0:T(8,128)(2,1)} %get-tuple-element.12.so_in, bf16[128,4096]{1,0:T(8,128)(2,1)} %get-tuple-element.13.qg_in, bf16[128,512]{1,0:T(8,128)(2,1)} %get-tuple-element.14.kg_in, ...), custom_call_target="tpu_custom_call" | custom-call | tf_op jit(solution)/shard_map/pallas_call | solution.py:476

commit v4 on v3

--- a/solution.py
+++ b/solution.py
@@ -40,8 +40,8 @@
 
 def _kernel(
     sizes,
-    plan_ref,
-    seg_ref,
+    plan_hbm,
+    seg_hbm,
     q_hbm,
     k_hbm,
     v_hbm,
@@ -50,6 +50,8 @@
     qg_out,
     kg_out,
     vg_out,
+    plan_ref,
+    seg_ref,
     kv,
     qb,
     dob,
@@ -125,6 +127,29 @@
             do_hbm.at[:, pl.ds(pl.multiple_of(g * width, width), width)], dob.at[g], loc_sem.at[3, g]
         )
 
+    barrier = pltpu.get_barrier_semaphore()
+    not_first, not_last = p > 0, p < n_pipe - 1
+
+    def signal(semaphore, target):
+        pl.semaphore_signal(semaphore, inc=1, device_id=target, device_id_type=MESH)
+
+    for target in (other, down1, down2):
+        signal(barrier, target)
+
+    @pl.when(d == 0)
+    def _():
+        signal(barrier, across)
+
+    @pl.when(not_last)
+    def _():
+        signal(barrier, later)
+
+    @pl.when(not_first)
+    def _():
+        signal(barrier, earlier)
+
+    plan_copy = pltpu.make_async_copy(plan_hbm, plan_ref, loc_sem.at[4, 0])
+    seg_copy = pltpu.make_async_copy(seg_hbm, seg_ref, loc_sem.at[4, 1])
     for g in range(groups):
         for copy in own_kv(g):
             copy.start()
@@ -132,27 +157,8 @@
         own_q(g).start()
     for g in range(groups):
         own_do(g).start()
-
-    barrier = pltpu.get_barrier_semaphore()
-    not_first, not_last = p > 0, p < n_pipe - 1
-
-    def signal(semaphore, target):
-        pl.semaphore_signal(semaphore, inc=1, device_id=target, device_id_type=MESH)
-
-    for target in (other, down1, down2):
-        signal(barrier, target)
-
-    @pl.when(d == 0)
-    def _():
-        signal(barrier, across)
-
-    @pl.when(not_last)
-    def _():
-        signal(barrier, later)
-
-    @pl.when(not_first)
-    def _():
-        signal(barrier, earlier)
+    plan_copy.start()
+    seg_copy.start()
 
     for g in range(groups):
         for copy in own_kv(g):
@@ -210,6 +216,8 @@
 
     q_other(0).start()
 
+    plan_copy.wait()
+    seg_copy.wait()
     zeros = jnp.zeros((pad, 2 * HEAD_SIZE), F32)
     shifts = []
     row_at = lax.broadcasted_iota(jnp.int32, seg_ref.shape, 0)
@@ -293,6 +301,8 @@
         total = loc[g, 1] + back[g, 2].astype(F32) + back[g, 3].astype(F32)
         psend[g] = total.astype(BF16)
         fin_copy(g).start()
+
+    behind = (lax.rem(p, 4) == 1) | (lax.rem(p, 4) == 2)
 
     def one_group(g, carry):
         for kind in range(1, 5):
@@ -331,22 +341,32 @@
         for kind in range(4):
             ret_copy(g, kind).start()
 
-        @pl.when(not_last)
+        @pl.when(not_last & ((g < groups - 1) | jnp.logical_not(behind)))
         def _():
             att_copy(g).start()
 
-        @pl.when(not_first)
+        @pl.when(not_first & ((g < groups - 1) | jnp.logical_not(behind)))
         def _():
             dq_copy(g).start()
 
-        @pl.when(g > 0)
+        @pl.when(g > 1)
         def _():
-            pass_on(g - 1)
+            pass_on(g - 2)
 
         return carry
 
     lax.fori_loop(0, groups, one_group, 0)
+    pass_on(groups - 2)
     pass_on(groups - 1)
+
+    @pl.when(not_last & behind)
+    def _():
+        att_copy(groups - 1).start()
+
+    @pl.when(not_first & behind)
+    def _():
+        dq_copy(groups - 1).start()
+
 
     def finish(g, carry):
         fin_copy(g).wait_recv()
@@ -382,40 +402,37 @@
     lax.fori_loop(0, groups, drain, 0)
 
 
-def _place(sizes, so_in, qg_in, kg_in, vg_in, so_out, qg_out, kg_out, vg_out, so, qg, kg, vg, in_sem, out_sem):
+def _place(sizes, so_in, qg_in, kg_in, vg_in, so_out, qg_out, kg_out, vg_out, empty, sem):
     p = lax.axis_index("pipe")
-    moves = []
-    for source, buffer, to, none in (
-        (so_in, so, so_out, 0),
-        (qg_in, qg, qg_out, sizes[0] - 1),
-        (kg_in, kg, kg_out, None),
-        (vg_in, vg, vg_out, None),
-    ):
-        pieces = 1 if none is None else PIECES
-        step = source.shape[0] // pieces
-        for k in range(pieces):
-            part, n = pl.ds(k * step, step), len(moves)
-            moves.append(
-                (
-                    pltpu.make_async_copy(source.at[part], buffer.at[part], in_sem.at[n]),
-                    pltpu.make_async_copy(buffer.at[part], to.at[part], out_sem.at[n]),
-                    none,
-                    buffer.at[part],
-                )
-            )
-    for load, _, _, _ in moves:
-        load.start()
-    for load, store, none, buffer in moves:
-        load.wait()
-        if none is not None:
-
-            @pl.when(p == none)
-            def _(buffer=buffer):
-                buffer[...] = jnp.zeros(buffer.shape, buffer.dtype)
-
-        store.start()
-    for _, store, _, _ in moves:
-        store.wait()
+    step = so_in.shape[0] // PIECES
+
+    def pieces(source, to, first):
+        return [
+            pltpu.make_async_copy(source.at[pl.ds(k * step, step)], to.at[pl.ds(k * step, step)], sem.at[first + k])
+            for k in range(PIECES)
+        ]
+
+    small = [
+        pltpu.make_async_copy(kg_in, kg_out, sem.at[2 * PIECES]),
+        pltpu.make_async_copy(vg_in, vg_out, sem.at[2 * PIECES + 1]),
+    ]
+    for source, to, first, none in ((so_in, so_out, 0, 0), (qg_in, qg_out, PIECES, sizes[0] - 1)):
+
+        @pl.when(p != none)
+        def _(source=source, to=to, first=first):
+            for copy in pieces(source, to, first):
+                copy.start()
+
+        @pl.when(p == none)
+        def _(to=to, first=first):
+            empty[...] = jnp.zeros_like(empty)
+            for copy in pieces(empty, to, first):
+                copy.start()
+
+    for copy in small:
+        copy.start()
+    for copy in pieces(so_in, so_out, 0) + pieces(qg_in, qg_out, PIECES) + small:
+        copy.wait()
 
 
 def _on_device(sizes, section_queries, section_keys, cascade_value_rows, output_grad, segments, stretch_plan):
@@ -429,14 +446,16 @@
     attended, query_grad, key_grad, value_grad = pl.pallas_call(
         functools.partial(_kernel, sizes),
         out_shape=[
-            jax.ShapeDtypeStruct((rows, width), BF16),
-            jax.ShapeDtypeStruct((rows, width), BF16),
-            jax.ShapeDtypeStruct((rows, kv_width), BF16),
-            jax.ShapeDtypeStruct((rows, kv_width), BF16),
+            pltpu.VMEM((rows, width), BF16),
+            pltpu.VMEM((rows, width), BF16),
+            pltpu.VMEM((rows, kv_width), BF16),
+            pltpu.VMEM((rows, kv_width), BF16),
         ],
-        in_specs=[pl.BlockSpec(memory_space=pltpu.SMEM), vmem, hbm, hbm, hbm, hbm],
-        out_specs=[hbm, hbm, vmem, vmem],
+        in_specs=[hbm] * 6,
+        out_specs=[vmem] * 4,
         scratch_shapes=[
+            pltpu.SMEM(stretch_plan.shape, jnp.int32),
+            pltpu.VMEM((segments.shape[0] // rows, rows), jnp.int32),
             pltpu.VMEM((groups, 6 * rows, 2 * HEAD_SIZE), BF16),
             pltpu.VMEM((groups, 2 * rows, share), BF16),
             pltpu.VMEM((groups, rows, share), BF16),
@@ -449,7 +468,7 @@
             pltpu.VMEM((groups, 4, rows, 2 * HEAD_SIZE), BF16),
             pltpu.VMEM((groups, rows, 2 * HEAD_SIZE), BF16),
             pltpu.VMEM((groups, rows, 2 * HEAD_SIZE), BF16),
-            dma((4, groups)),
+            dma((5, groups)),
             dma((5, groups)),
             dma((5, groups)),
             dma((2, groups)),
@@ -463,15 +482,20 @@
             pltpu.SemaphoreType.REGULAR((3,)),
         ],
         compiler_params=pltpu.CompilerParams(
-            collective_id=0, has_side_effects=True, vmem_limit_bytes=56 * 1024 * 1024
+            collective_id=0, has_side_effects=True, vmem_limit_bytes=40 * 1024 * 1024
         ),
     )(
-        stretch_plan,
-        segments.reshape(-1, rows),
-        section_queries[0],
-        section_keys[0],
-        cascade_value_rows[0],
-        output_grad[0],
+        *(
+            pltpu.with_memory_space_constraint(value, pltpu.HBM)
+            for value in (
+                stretch_plan,
+                segments.reshape(-1, rows),
+                section_queries[0],
+                section_keys[0],
+                cascade_value_rows[0],
+                output_grad[0],
+            )
+        )
     )
     section_output, query_grad_sent, key_grad, value_grad = pl.pallas_call(
         functools.partial(_place, sizes),
@@ -481,17 +505,10 @@
             jax.ShapeDtypeStruct((rows, kv_width), BF16),
             jax.ShapeDtypeStruct((rows, kv_width), BF16),
         ],
-        in_specs=[hbm] * 4,
+        in_specs=[vmem] * 4,
         out_specs=[hbm] * 4,
-        scratch_shapes=[
-            pltpu.VMEM((rows, width), BF16),
-            pltpu.VMEM((rows, width), BF16),
-            pltpu.VMEM((rows, kv_width), BF16),
-            pltpu.VMEM((rows, kv_width), BF16),
-            dma((2 * PIECES + 2,)),
-            dma((2 * PIECES + 2,)),
-        ],
-        compiler_params=pltpu.CompilerParams(vmem_limit_bytes=56 * 1024 * 1024),
+        scratch_shapes=[pltpu.VMEM((rows, width), BF16), dma((2 * PIECES + 2,))],
+        compiler_params=pltpu.CompilerParams(vmem_limit_bytes=16 * 1024 * 1024),
     )(attended, query_grad, key_grad, value_grad)
     return section_output[None], query_grad_sent[None], key_grad[None], value_grad[None]
 

time: 97.6 us -> 95.2 us (0.975)
  Pallas kernels: 96.4 us -> 94.4 us
    pallas_call x1, Pallas kernels: 2.51 us -> 1.49 us  [_on_device(): pl.pallas_call(functools.partial(_place, sizes), out_shape=[jax.ShapeDtyp...]
    pallas_call x1, Pallas kernels: 93.9 us -> 92.9 us  [_on_device(): pl.pallas_call(functools.partial(_kernel, sizes), out_shape=[pltpu.VMEM((...]
where the time goes in v4:
time: 95.2 us; the launch traced here: 95 us
  Pallas kernels  94.4 us (99%)
    pallas_call x1, Pallas kernels, _on_device(): pl.pallas_call(functools.partial(_kernel, sizes), out_shape=[pltpu.VMEM((...  92.9 us

profile of v4, /device:TPU:1, one launch (start us, length us, event | category | flops | bytes accessed | tf_op | source)
XLA Modules:
  0.0 95.0 jit_solution(5559811175903688792)
XLA Ops:
  0.6 92.9 %shard_map.93 = (bf16[128,4096]{1,0:T(8,128)(2,1)S(1)}, bf16[128,4096]{1,0:T(8,128)(2,1)S(1)}, bf16[128,512]{1,0:T(8,128)(2,1)S(1)}, bf16[128,512]{1,0:T(8,128)(2,1)S(1)}) custom-call(s32[128]{0:T(128)} %plan_hbm.1, s32[64,128]{1,0:T(8,128)} %bitcast.13, bf16[128,4096]{1,0:T(8,128)(2,1)} %bitcast.9, bf16[128,512]{1,0:T(8,128)(2,1)} %bitcast.11, ...), custom_call_target="tpu_custom_call" | custom-call | tf_op jit(solution)/shard_map/pallas_call | solution.py:446
  93.5 1.5 %shard_map.94 = (bf16[128,4096]{1,0:T(8,128)(2,1)}, bf16[128,4096]{1,0:T(8,128)(2,1)}, bf16[128,512]{1,0:T(8,128)(2,1)}, bf16[128,512]{1,0:T(8,128)(2,1)}) custom-call(bf16[128,4096]{1,0:T(8,128)(2,1)S(1)} %get-tuple-element.12.so_in, bf16[128,4096]{1,0:T(8,128)(2,1)S(1)} %get-tuple-element.13.qg_in, bf16[128,512]{1,0:T(8,128)(2,1)S(1)} %get-tuple-element.14.kg_in, ...), custom_call_target="tpu_custom_call" | custom-call | tf_op jit(solution)/shard_map/pallas_call | solution.py:500

commit v5 on v4

--- a/solution.py
+++ b/solution.py
@@ -296,7 +296,7 @@
         return total
 
     def pass_on(g):
-        for kind in range(4):
+        for kind in (3, 2):
             ret_copy(g, kind).wait_recv()
         total = loc[g, 1] + back[g, 2].astype(F32) + back[g, 3].astype(F32)
         psend[g] = total.astype(BF16)
@@ -338,7 +338,7 @@
             ret[g, o] = window_part(o).astype(BF16)
         loc[g, 0] = window_part(4)
         loc[g, 1] = window_part(5 - 2 * d)
-        for kind in range(4):
+        for kind in (3, 2, 0, 1):
             ret_copy(g, kind).start()
 
         @pl.when(not_last & ((g < groups - 1) | jnp.logical_not(behind)))
@@ -349,14 +349,13 @@
         def _():
             dq_copy(g).start()
 
-        @pl.when(g > 1)
+        @pl.when(g > 0)
         def _():
-            pass_on(g - 2)
+            pass_on(g - 1)
 
         return carry
 
     lax.fori_loop(0, groups, one_group, 0)
-    pass_on(groups - 2)
     pass_on(groups - 1)
 
     @pl.when(not_last & behind)
@@ -369,6 +368,8 @@
 
 
     def finish(g, carry):
+        for kind in (0, 1):
+            ret_copy(g, kind).wait_recv()
         fin_copy(g).wait_recv()
         total = loc[g, 0] + back[g, 0].astype(F32) + back[g, 1].astype(F32) + precv[g].astype(F32)
         place = pl.ds(pl.multiple_of(g * HEAD_SIZE, HEAD_SIZE), HEAD_SIZE)

time: 95.2 us -> 93.6 us (0.983)
  Pallas kernels: 94.4 us -> 92.8 us
    pallas_call x1, Pallas kernels: 92.9 us -> 91.3 us  [_on_device(): pl.pallas_call(functools.partial(_kernel, sizes), out_shape=[pltpu.VMEM((...]
where the time goes in v5:
time: 93.6 us; the launch traced here: 93.4 us
  Pallas kernels  92.8 us (99%)
    pallas_call x1, Pallas kernels, _on_device(): pl.pallas_call(functools.partial(_kernel, sizes), out_shape=[pltpu.VMEM((...  91.3 us

profile of v5, /device:TPU:1, one launch (start us, length us, event | category | flops | bytes accessed | tf_op | source)
XLA Modules:
  0.0 93.4 jit_solution(9642211389680749589)
XLA Ops:
  0.6 91.3 %shard_map.93 = (bf16[128,4096]{1,0:T(8,128)(2,1)S(1)}, bf16[128,4096]{1,0:T(8,128)(2,1)S(1)}, bf16[128,512]{1,0:T(8,128)(2,1)S(1)}, bf16[128,512]{1,0:T(8,128)(2,1)S(1)}) custom-call(s32[128]{0:T(128)} %plan_hbm.1, s32[64,128]{1,0:T(8,128)} %bitcast.13, bf16[128,4096]{1,0:T(8,128)(2,1)} %bitcast.9, bf16[128,512]{1,0:T(8,128)(2,1)} %bitcast.11, ...), custom_call_target="tpu_custom_call" | custom-call | tf_op jit(solution)/shard_map/pallas_call | solution.py:447
  91.9 1.5 %shard_map.94 = (bf16[128,4096]{1,0:T(8,128)(2,1)}, bf16[128,4096]{1,0:T(8,128)(2,1)}, bf16[128,512]{1,0:T(8,128)(2,1)}, bf16[128,512]{1,0:T(8,128)(2,1)}) custom-call(bf16[128,4096]{1,0:T(8,128)(2,1)S(1)} %get-tuple-element.12.so_in, bf16[128,4096]{1,0:T(8,128)(2,1)S(1)} %get-tuple-element.13.qg_in, bf16[128,512]{1,0:T(8,128)(2,1)S(1)} %get-tuple-element.14.kg_in, ...), custom_call_target="tpu_custom_call" | custom-call | tf_op jit(solution)/shard_map/pallas_call | solution.py:501

commit v6 on v5

--- a/solution.py
+++ b/solution.py
@@ -129,16 +129,27 @@
 
     barrier = pltpu.get_barrier_semaphore()
     not_first, not_last = p > 0, p < n_pipe - 1
+    has_up1, has_up2, has_down1, has_down2 = c < n_ctx - 1, c < n_ctx - 2, c > 0, c > 1
+    low, high = d == 0, d == 1
+    side = (low & has_down1) | (high & has_up1)
+    far_out = (low & has_up2) | (high & has_down1)
+    far_in = (low & has_down2) | (high & has_up1)
+    kv_out, kv_in = (None, has_up1, has_up2, has_up1, far_out), (None, has_down1, has_down2, has_down1, far_in)
+    ret_out, ret_in = (has_down2, has_down1, has_down1, far_in), (has_up2, has_up1, has_up1, far_out)
+
+    def when(condition, action):
+        if condition is None:
+            action()
+        else:
+            pl.when(condition)(action)
 
     def signal(semaphore, target):
         pl.semaphore_signal(semaphore, inc=1, device_id=target, device_id_type=MESH)
 
-    for target in (other, down1, down2):
-        signal(barrier, target)
-
-    @pl.when(d == 0)
-    def _():
-        signal(barrier, across)
+    signal(barrier, other)
+    when(has_down1, lambda: signal(barrier, down1))
+    when(has_down2, lambda: signal(barrier, down2))
+    when(low & has_down1, lambda: signal(barrier, across))
 
     @pl.when(not_last)
     def _():
@@ -164,13 +175,13 @@
         for copy in own_kv(g):
             copy.wait()
         own_q(g).wait()
-    pl.semaphore_wait(barrier, 3 + d + not_last.astype(jnp.int32) + not_first.astype(jnp.int32))
-    signal(hello.at[0], up1)
-    signal(hello.at[1], up2)
-
-    @pl.when(d == 1)
-    def _():
-        signal(hello.at[2], across)
+    expected = 1
+    for condition in (has_up1, has_up2, high & has_up1, not_last, not_first):
+        expected = expected + condition.astype(jnp.int32)
+    pl.semaphore_wait(barrier, expected)
+    when(has_up1, lambda: signal(hello.at[0], up1))
+    when(has_up2, lambda: signal(hello.at[1], up2))
+    when(high & has_up1, lambda: signal(hello.at[2], across))
 
 
     def kv_copy(kind, g):
@@ -211,8 +222,8 @@
 
     for g in range(groups):
         kv_copy(0, g).start()
-    kv_copy(1, 0).start()
-    kv_copy(2, 0).start()
+    when(kv_out[1], lambda: kv_copy(1, 0).start())
+    when(kv_out[2], lambda: kv_copy(2, 0).start())
 
     q_other(0).start()
 
@@ -244,26 +255,34 @@
         parts[s, pl.ds(0, pad)] = zeros
         parts[s, pl.ds(pad + window, pad + rows - half)] = jnp.zeros((pad + rows - half, 2 * HEAD_SIZE), F32)
 
-    @pl.when(d == 0)
-    def _():
-        pl.semaphore_wait(hello.at[2], 1)
-
-    q_across(0).start()
+    when(low & has_down1, lambda: pl.semaphore_wait(hello.at[2], 1))
+    when(side, lambda: q_across(0).start())
     for g in range(1, groups):
         q_other(g).start()
-        q_across(g).start()
-    pl.semaphore_wait(hello.at[0], 1)
-    pl.semaphore_wait(hello.at[1], 1)
+        when(side, lambda g=g: q_across(g).start())
+    when(has_down1, lambda: pl.semaphore_wait(hello.at[0], 1))
+    when(has_down2, lambda: pl.semaphore_wait(hello.at[1], 1))
+
+    def clear_rows(kind):
+        place = (0, 2, 0, 3 - 2 * d, 1 + 4 * d)[kind]
+        for g in range(groups):
+            kv[g, pl.ds(pl.multiple_of(place * rows, rows), rows)] = jnp.zeros((rows, 2 * HEAD_SIZE), BF16)
+
+    def clear_back(kind):
+        for g in range(groups):
+            back[g, kind] = jnp.zeros((rows, 2 * HEAD_SIZE), BF16)
+
+    for kind in range(1, 5):
+        when(jnp.logical_not(kv_in[kind]), lambda kind=kind: clear_rows(kind))
+    for kind in range(4):
+        when(jnp.logical_not(ret_in[kind]), lambda kind=kind: clear_back(kind))
 
     def relay(g, carry):
         kv_copy(0, g).wait_recv()
-        kv_copy(3, g).start()
-        kv_copy(4, g).start()
-
-        @pl.when(g + 1 < groups)
-        def _():
-            kv_copy(1, g + 1).start()
-            kv_copy(2, g + 1).start()
+        when(kv_out[3], lambda: kv_copy(3, g).start())
+        when(kv_out[4], lambda: kv_copy(4, g).start())
+        when(kv_out[1] & (g + 1 < groups), lambda: kv_copy(1, g + 1).start())
+        when(kv_out[2] & (g + 1 < groups), lambda: kv_copy(2, g + 1).start())
 
         return carry
 
@@ -297,18 +316,18 @@
 
     def pass_on(g):
         for kind in (3, 2):
-            ret_copy(g, kind).wait_recv()
+            when(ret_in[kind], lambda kind=kind: ret_copy(g, kind).wait_recv())
         total = loc[g, 1] + back[g, 2].astype(F32) + back[g, 3].astype(F32)
         psend[g] = total.astype(BF16)
         fin_copy(g).start()
 
-    behind = (lax.rem(p, 4) == 1) | (lax.rem(p, 4) == 2)
+    behind = (d == 1) & ((lax.rem(p, 4) == 1) | (lax.rem(p, 4) == 2))
 
     def one_group(g, carry):
         for kind in range(1, 5):
-            kv_copy(kind, g).wait_recv()
+            when(kv_in[kind], lambda kind=kind: kv_copy(kind, g).wait_recv())
         q_other(g).wait_recv()
-        q_across(g).wait_recv()
+        when(side, lambda: q_across(g).wait_recv())
         for s in range(2):
             shift = shifts[s]
             chosen = one_of(shift, [qb[g, pl.ds(k * half, half), :] for k in range(4)])
@@ -339,7 +358,7 @@
         loc[g, 0] = window_part(4)
         loc[g, 1] = window_part(5 - 2 * d)
         for kind in (3, 2, 0, 1):
-            ret_copy(g, kind).start()
+            when(ret_out[kind], lambda kind=kind: ret_copy(g, kind).start())
 
         @pl.when(not_last & ((g < groups - 1) | jnp.logical_not(behind)))
         def _():
@@ -369,7 +388,7 @@
 
     def finish(g, carry):
         for kind in (0, 1):
-            ret_copy(g, kind).wait_recv()
+            when(ret_in[kind], lambda kind=kind: ret_copy(g, kind).wait_recv())
         fin_copy(g).wait_recv()
         total = loc[g, 0] + back[g, 0].astype(F32) + back[g, 1].astype(F32) + precv[g].astype(F32)
         place = pl.ds(pl.multiple_of(g * HEAD_SIZE, HEAD_SIZE), HEAD_SIZE)
@@ -381,11 +400,11 @@
 
     def drain(g, carry):
         for kind in range(5):
-            kv_copy(kind, g).wait_send()
+            when(kv_out[kind], lambda kind=kind: kv_copy(kind, g).wait_send())
         q_other(g).wait_send()
-        q_across(g).wait_send()
+        when(side, lambda: q_across(g).wait_send())
         for kind in range(4):
-            ret_copy(g, kind).wait_send()
+            when(ret_out[kind], lambda kind=kind: ret_copy(g, kind).wait_send())
         fin_copy(g).wait_send()
 
         @pl.when(not_last)

time: 93.6 us -> 91.8 us (0.981)
  the two profiles are of different devices: /device:TPU:1 before, /device:TPU:190 now
where the time goes in v6:
time: 91.8 us; the launch traced here: 91.6 us
  Pallas kernels  91 us (99%)
    pallas_call x1, Pallas kernels, _on_device(): pl.pallas_call(functools.partial(_kernel, sizes), out_shape=[pltpu.VMEM((...  89.5 us

profile of v6, /device:TPU:190, one launch (start us, length us, event | category | flops | bytes accessed | tf_op | source)
XLA Modules:
  0.0 91.6 jit_solution(8917603337693205092)
XLA Ops:
  0.6 89.5 %shard_map.93 = (bf16[128,4096]{1,0:T(8,128)(2,1)S(1)}, bf16[128,4096]{1,0:T(8,128)(2,1)S(1)}, bf16[128,512]{1,0:T(8,128)(2,1)S(1)}, bf16[128,512]{1,0:T(8,128)(2,1)S(1)}) custom-call(s32[128]{0:T(128)} %plan_hbm.1, s32[64,128]{1,0:T(8,128)} %bitcast.13, bf16[128,4096]{1,0:T(8,128)(2,1)} %bitcast.9, bf16[128,512]{1,0:T(8,128)(2,1)} %bitcast.11, ...), custom_call_target="tpu_custom_call" | custom-call | tf_op jit(solution)/shard_map/pallas_call | solution.py:466
  90.2 1.5 %shard_map.94 = (bf16[128,4096]{1,0:T(8,128)(2,1)}, bf16[128,4096]{1,0:T(8,128)(2,1)}, bf16[128,512]{1,0:T(8,128)(2,1)}, bf16[128,512]{1,0:T(8,128)(2,1)}) custom-call(bf16[128,4096]{1,0:T(8,128)(2,1)S(1)} %get-tuple-element.12.so_in, bf16[128,4096]{1,0:T(8,128)(2,1)S(1)} %get-tuple-element.13.qg_in, bf16[128,512]{1,0:T(8,128)(2,1)S(1)} %get-tuple-element.14.kg_in, ...), custom_call_target="tpu_custom_call" | custom-call | tf_op jit(solution)/shard_map/pallas_call | solution.py:520
